TPU v7x, 32 devices: a whole 2x2x4 slice. The times are simulated.
32 devices in a mesh: tower: 2 (over core), dp: 16 (over z, y, x).
Axes of the slice: x: 2, y: 2, z: 4, core: 2. Of those that a mesh axis runs over, the one named last changes fastest.
Arguments:
- block_input: bfloat16 [2, 17280, 768], P('tower', 'dp'), may hold values from -6 to 6
- segments: int32 [224, 77], P('dp'), may hold values from 0 to 19, as said below
- caption_ends: int32 [320], P('dp'), may hold values from 15 to 1077, as said below
- pair_flags: int32 [320], replicated, may hold values from 0 to 1, as said below
- attention_gain: float32 [2, 768], P('tower'), may hold values from 0.1 to 1.9
- attention_bias: float32 [2, 768], P('tower'), may hold values from -3 to 3
- triple_weight: bfloat16 [2, 3, 768, 768], P('tower'), may hold values from -0.21875 to 0.21875
- triple_bias: float32 [2, 2, 768], P('tower'), may hold values from -3 to 3
- mixer_weight: bfloat16 [2, 768, 768], P('tower'), may hold values from -1.25 to 1.25
- mixer_bias: float32 [2, 768], P('tower'), may hold values from -3 to 3
- feed_gain: float32 [2, 768], P('tower'), may hold values from 0.1 to 1.9
- feed_bias: float32 [2, 768], P('tower'), may hold values from -3 to 3
- widen_weight: bfloat16 [2, 768, 3072], P('tower'), may hold values from -0.21875 to 0.21875
- widen_bias: float32 [2, 3072], P('tower'), may hold values from -3 to 3
- narrow_weight: bfloat16 [2, 3072, 768], P('tower'), may hold values from -0.15625 to 0.15625
- narrow_bias: float32 [2, 768], P('tower'), may hold values from -3 to 3
- final_gain: float32 [2, 768], P('tower'), may hold values from 0.1 to 1.9
- final_bias: float32 [2, 768], P('tower'), may hold values from -3 to 3
- embed_weight: bfloat16 [2, 768, 512], P('tower'), may hold values from -0.21875 to 0.21875
- logit_scale: float32 [], replicated, may hold values from 3.6 to 4.4
- loss_scale: float32 [], replicated, may hold values from 160 to 640
Outputs:
- mean_loss: float32 [], replicated
- accuracy: float32 [], replicated
- block_input_gradient: float32 [2, 17280, 768], P('tower', 'dp')
- attention_gain_gradient: float32 [2, 768], P('tower', 'dp')
- attention_bias_gradient: float32 [2, 768], P('tower', 'dp')
- triple_weight_gradient: float32 [2, 3, 768, 768], P('tower', None, 'dp')
- triple_bias_gradient: float32 [2, 2, 768], P('tower', None, 'dp')
- mixer_weight_gradient: float32 [2, 768, 768], P('tower', 'dp')
- mixer_bias_gradient: float32 [2, 768], P('tower', 'dp')
- feed_gain_gradient: float32 [2, 768], P('tower', 'dp')
- feed_bias_gradient: float32 [2, 768], P('tower', 'dp')
- widen_weight_gradient: float32 [2, 768, 3072], P('tower', None, 'dp')
- widen_bias_gradient: float32 [2, 3072], P('tower', 'dp')
- narrow_weight_gradient: float32 [2, 3072, 768], P('tower', 'dp')
- narrow_bias_gradient: float32 [2, 768], P('tower', 'dp')
- final_gain_gradient: float32 [2, 768], P('tower', 'dp')
- final_bias_gradient: float32 [2, 768], P('tower', 'dp')
- embed_weight_gradient: float32 [2, 768, 512], P('tower', 'dp')
- logit_scale_gradient: float32 [], replicated
Inputs may be any that keep to these rules, and one draw needn't show every extreme that they name: `segments`: the 14 caption rows of each dp index hold captions 0 to 19 in order, one or two whole captions a row, each of 16 to 77 tokens; caption k of dp index d is pair d * 20 + k. caption_ends[c] is the last position, counted over the 1078 tokens of its dp index, where segments holds c mod 20. `pair_flags`: the last pair is real.
All inputs are finite; a program needn't handle non-finite values.
Results may differ from a plain program's by a relative error of at most 0.024.
Values may be sent and summed in bfloat16 or wider, within the bound.
No kernel may reach another device: no remote copies, remote signals or barrier semaphores. Data moves between devices by JAX's collectives and lax.ppermute only.
A program may use at most 256 MiB of HBM per device.

v0:
```python
from functools import partial

import jax
import jax.numpy as jnp
from jax import lax
from jax.experimental import pallas as pl
from jax.experimental.pallas import tpu as pltpu
from jax.sharding import PartitionSpec as P

D_TXT = 512
MLP_TXT = 2048
HEAD = 64
IMG_TOK = 50
CTX = 77
F32 = jnp.float32
BF16 = jnp.bfloat16
VMEM_LIMIT = 62 * 1024 * 1024
CHUNK = 1024
NORM_ROWS = 272
PROJECT_ROWS = 1088


def dot_dims(left, right, left_dim, right_dim, precision=None):
    return lax.dot_general(
        left,
        right,
        (((left_dim,), (right_dim,)), ((), ())),
        preferred_element_type=F32,
        precision=precision,
    )


def mm(left, right):
    return dot_dims(left, right, 1, 0)


def mm_nt(left, right):
    return dot_dims(left, right, 1, 1)


def mm_tn(left, right):
    return dot_dims(left, right, 0, 0)


def iota(shape, dim):
    return lax.broadcasted_iota(jnp.int32, shape, dim)


def sigmoid(rows):
    return 1.0 / (1.0 + jnp.exp(-rows))


def one_hot(condition):
    return condition.astype(F32).astype(BF16)


def normed(rows, mask, width):
    mean = jnp.sum(rows * mask, axis=-1, keepdims=True) / width
    centre = (rows - mean) * mask
    invert = lax.rsqrt(jnp.sum(centre * centre, axis=-1, keepdims=True) / width + 1e-05)
    return centre * invert, invert


def norm_back(rows_hat, invert, gain, upward, mask, width):
    scaled = upward * gain
    mean = jnp.sum(scaled, axis=-1, keepdims=True) / width
    along = jnp.sum(scaled * rows_hat, axis=-1, keepdims=True) / width
    return invert * (scaled - mean * mask - rows_hat * along)


def sums_of(rows):
    return jnp.sum(rows, axis=0, keepdims=True)


def head_mask(rows, pairs, width):
    row = iota((rows, width), 0)
    first = lax.shift_right_logical(iota((rows, width), 1), 6) * pairs
    return (row >= first) & (row < first + pairs)


def repeat_rows(rows, pairs):
    row = iota((rows, pairs), 0)
    return one_hot(lax.rem(row, pairs) == iota((rows, pairs), 1))


def tower_sizes(full_width, full_hidden):
    is_text = lax.axis_index("tower") != 0
    width = jnp.where(is_text, D_TXT, full_width)
    mask = (iota((1, full_width), 1) < width).astype(F32)
    return is_text, width.astype(F32), mask


def fetch(source, target, semaphore):
    copy = pltpu.make_async_copy(source, target, semaphore)
    copy.start()
    return copy


def three_parts(rows):
    parts = []
    for _ in range(3):
        part = rows.astype(BF16).astype(F32)
        parts.append(part)
        rows = rows - part
    return jnp.concatenate(parts, axis=0).astype(BF16)


def over_tokens(tokens, size, step):
    for at in range(0, tokens, size):
        step(at, min(size, tokens - at))


def across(lane_sums, full_width):
    return jnp.concatenate([lane_sums] * (full_width // 128), axis=1)


def pooled_spots(ends_ref, is_text, pairs, copies):
    pair = lax.rem(iota((copies * pairs, pairs), 0), pairs)
    ends = jnp.where(pair == iota((copies * pairs, pairs), 1), ends_ref[...], 0).astype(F32)
    ends = jnp.sum(ends, axis=1, keepdims=True)
    firsts = (lax.rem(iota((copies * pairs, 1), 0), pairs) * IMG_TOK).astype(F32)
    return jnp.where(is_text, ends, firsts)


def embed_back(embedded, grad_unit):
    inv_norm = lax.rsqrt(jnp.sum(embedded * embedded, axis=-1, keepdims=True) + 1e-06)
    along = jnp.sum(embedded * grad_unit, axis=-1, keepdims=True)
    return (inv_norm * grad_unit - inv_norm * inv_norm * inv_norm * embedded * along).astype(BF16)


class Hidden:
    def __init__(self, widen_hbm, narrow_hbm, s_widen, s_narrow, sems, chunks):
        self.pairs = (
            (lambda at: widen_hbm.at[0, :, pl.ds(at, CHUNK)], lambda at: s_widen.at[:, pl.ds(at, CHUNK)]),
            (lambda at: narrow_hbm.at[0, pl.ds(at, CHUNK), :], lambda at: s_narrow.at[pl.ds(at, CHUNK), :]),
        )
        self.sems = sems
        self.chunks = chunks

    def copy(self, which, chunk):
        source, target = self.pairs[which]
        at = chunk * CHUNK
        if not isinstance(at, int):
            at = pl.multiple_of(at, CHUNK)
        return pltpu.make_async_copy(source(at), target(at), self.sems.at[which, chunk])

    def start(self, order):
        for chunk in range(self.chunks):
            for which in order:
                self.copy(which, chunk).start()

    def wait(self, chunk):
        self.copy(0, chunk).wait()
        self.copy(1, chunk).wait()

    def each(self, step):
        for chunk in range(self.chunks):
            self.wait(chunk)
            step(slice(chunk * CHUNK, (chunk + 1) * CHUNK))


def attend_kernel(
    dims,
    ends_ref,
    x_hbm,
    ag,
    ab,
    triple_hbm,
    triple_bias,
    wo_hbm,
    bo,
    fg,
    fb,
    ww_hbm,
    bw,
    wn_hbm,
    bn,
    lg,
    lb,
    we_hbm,
    unit_ref,
    early_ref,
    hat_hbm,
    inv_hbm,
    probs_hbm,
    query_ref,
    embedded_ref,
    pooled_ref,
    middle_ref,
    slope_ref,
    s_x,
    s_one,
    s_hat,
    s_inv,
    s_probs,
    s_key,
    s_value,
    s_triple,
    s_wo,
    s_ww,
    s_wn,
    s_we,
    s_low,
    sems,
    hidden_sems,
):
    pairs, tokens, full_width, full_hidden = dims
    is_text, width, mask = tower_sizes(full_width, full_hidden)
    rows = full_width // HEAD * pairs
    get_x = fetch(x_hbm.at[0], s_x, sems.at[0])
    get_triple = fetch(triple_hbm.at[0], s_triple, sems.at[1])
    gain, shift = ag[...] * mask, ab[...] * mask
    ones = one_hot((iota((full_width, 128), 0)).astype(F32) < width)
    hidden = Hidden(ww_hbm, wn_hbm, s_ww, s_wn, hidden_sems, full_hidden // CHUNK)
    get_x.wait()
    get_wo = fetch(wo_hbm.at[0], s_wo, sems.at[2])
    hidden.start((0, 1))
    get_we = fetch(we_hbm.at[0], s_we, sems.at[3])

    def norm_rows(at, count):
        here = pl.ds(at, count)
        low = s_x[here, :]
        mean = mm(low, ones) / width
        centre = low.astype(F32) - across(mean, full_width)
        square = centre * centre
        high = square.astype(BF16)
        low = (square - high.astype(F32)).astype(BF16)
        invert = lax.rsqrt((mm(high, ones) + mm(low, ones)) / width + 1e-05)
        hat = centre * across(invert, full_width)
        s_hat[here, :] = hat.astype(BF16)
        s_one[here, :] = (hat * gain + shift).astype(BF16)
        s_inv[here, :] = invert

    over_tokens(tokens, NORM_ROWS, norm_rows)
    put_hat = fetch(s_hat, hat_hbm, sems.at[4])
    put_inv = fetch(s_inv, inv_hbm, sems.at[5])
    pick = one_hot(iota((pairs, tokens), 1).astype(F32) == pooled_spots(ends_ref, is_text, pairs, 1))
    stream_rows = mm(pick, s_x[...]) * mask
    one = mm(pick, s_one[...]).astype(BF16)
    get_triple.wait()
    query = ((mm(one, s_triple[0]) + triple_bias[0, 0:1, :]) * (mask * 0.125)).astype(BF16)
    repeat = repeat_rows(rows, pairs)
    heads = head_mask(rows, pairs, full_width)
    wide = jnp.where(heads, mm(repeat, query), 0.0).astype(BF16)

    def project(at, count):
        here = pl.ds(at, count)
        s_key[here, :] = mm(s_one[here, :], s_triple[1]).astype(BF16)
        s_value[here, :] = (mm(s_one[here, :], s_triple[2]) + triple_bias[0, 1:2, :]).astype(BF16)

    over_tokens(tokens, PROJECT_ROWS, project)
    s_probs[...] = mm_nt(wide, s_key[...])
    last = pooled_spots(ends_ref, is_text, pairs, rows // pairs)
    pair = lax.rem(iota((rows, 1), 0), pairs)
    stops = jnp.where(
        pair - 1 == iota((rows, pairs), 1), ends_ref[...] + 1, 0
    ).astype(F32)
    first = jnp.where(is_text, jnp.sum(stops, axis=1, keepdims=True), last)
    last = jnp.where(is_text, last, last + (IMG_TOK - 1.0))
    step_rows = 48
    for at in range(0, rows, step_rows):
        here = slice(at, at + step_rows)
        place = iota((step_rows, tokens), 1).astype(F32)
        allowed = (place >= first[here]) & (place <= last[here])
        scores = jnp.where(allowed, s_probs[here, :], -1e30)
        powers = jnp.exp(scores - jnp.max(scores, axis=1, keepdims=True))
        probs = powers * (1.0 / jnp.sum(powers, axis=1, keepdims=True))
        s_probs[here, :] = probs
        s_low[here, :] = probs.astype(BF16)
    put_probs = fetch(s_probs, probs_hbm, sems.at[6])
    mixed_wide = mm(s_low[...], s_value[...])
    mixed = mm_tn(repeat, jnp.where(heads, mixed_wide, 0.0).astype(BF16))
    mixed = (mixed * mask).astype(BF16)
    early_ref[:, 0:full_width] = mixed
    early_ref[:, full_width : 2 * full_width] = stream_rows.astype(BF16)
    get_wo.wait()
    middle = stream_rows + mm(mixed, s_wo[...]) + bo[...]
    middle_ref[...] = middle
    mid_hat, _ = normed(middle, mask, width)
    two = ((mid_hat * fg[...] + fb[...]) * mask).astype(BF16)
    pooled_ref[...] = middle + bn[...]
    hidden_width = jnp.where(is_text, MLP_TXT, full_hidden)
    hidden_mask = (iota((1, full_hidden), 1) < hidden_width).astype(F32)

    def forward(at):
        pre = mm(two, s_ww[:, at]) + bw[:, at]
        gate = sigmoid(1.702 * pre)
        active = pre * gate * hidden_mask[:, at]
        slope_ref[:, at] = (gate + 1.702 * active * (1.0 - gate)) * hidden_mask[:, at]
        pooled_ref[...] += mm(active.astype(BF16), s_wn[at, :])

    hidden.each(forward)
    out_hat, out_inv = normed(pooled_ref[...], mask, width)
    early_ref[:, 2 * full_width : 3 * full_width] = out_hat.astype(BF16)
    lane = iota((pairs, 128), 1)
    numbers = jnp.zeros((pairs, 128), F32)
    for place in range(3):
        part = out_inv.astype(BF16).astype(F32)
        numbers = jnp.where(lane == place, part, numbers)
        out_inv = out_inv - part
    early_ref[:, 3 * full_width :] = numbers.astype(BF16)
    three = ((out_hat * lg[...] + lb[...]) * mask).astype(BF16)
    get_we.wait()
    embedded = mm(three, s_we[...])
    embedded_ref[...] = embedded
    unit_ref[...] = (
        embedded * lax.rsqrt(jnp.sum(embedded * embedded, axis=-1, keepdims=True) + 1e-06)
    ).astype(BF16)
    query_ref[...] = query
    for copy in (put_hat, put_inv, put_probs):
        copy.wait()


def means_kernel(
    dims,
    ends_ref,
    ag,
    ab,
    hat_ref,
    probs_ref,
    query_ref,
    triple_hbm,
    turned_ref,
    spread_ref,
    keys_ref,
    hat_rows_ref,
    s_weight,
    s_turn,
    sems,
):
    pairs, tokens, full_width, full_hidden = dims
    is_text, width, mask = tower_sizes(full_width, full_hidden)
    get_weight = fetch(triple_hbm.at[0, 1], s_weight, sems.at[0])
    rows = probs_ref.shape[0]
    low = probs_ref[...].astype(BF16)
    spread = mm(low, hat_ref[...])
    spread_ref[...] = spread
    total = jnp.sum(low.astype(F32), axis=1, keepdims=True)
    s_turn[rows:, :] = jnp.zeros((s_turn.shape[0] - rows, full_width), F32)
    s_turn[0:rows, :] = (spread * ag[...] + total * ab[...]) * mask
    turned_ref[...] = s_turn[...].T.astype(BF16)
    pick = one_hot(iota((pairs, tokens), 1).astype(F32) == pooled_spots(ends_ref, is_text, pairs, 1))
    hat_rows_ref[...] = mm(pick, hat_ref[...]).astype(BF16)
    wide = mm(repeat_rows(rows, pairs), query_ref[...])
    wide = jnp.where(head_mask(rows, pairs, full_width), wide, 0.0).astype(BF16)
    get_weight.wait()
    keys_ref[...] = mm_nt(wide, s_weight[...]).astype(BF16)


def in_order(pieces, stages, pairs, block, at):
    here = lax.axis_index("dp")
    row = at + iota((block, 1), 0)
    owner = lax.div(row, pairs)
    apart = lax.bitwise_xor(owner, here)
    place = jnp.zeros_like(owner)
    weight = 1
    for shift, bits in stages:
        digit = lax.bitwise_and(lax.shift_right_logical(apart, shift), (1 << bits) - 1)
        place = place + digit * weight
        weight = weight << bits
    column = place * pairs + row - owner * pairs
    total = None
    first = 0
    for piece in pieces:
        count = piece.shape[0]
        part = mm(one_hot(iota((block, count), 1) + first == column), piece[...])
        total = part if total is None else total + part
        first += count
    return total.astype(BF16)


def over_blocks(count, step):
    if count == 1:
        step(0)
    else:

        def one(index, carry):
            step(index)
            return carry

        lax.fori_loop(0, count, one, 0)


def block_rows(total):
    return 320 if total % 320 == 0 else total


def loss_kernel(
    dims,
    own_rel,
    other_rel,
    flags_ref,
    logit_scale,
    loss_scale,
    ag,
    ab,
    triple_hbm,
    triple_bias,
    wo_hbm,
    fg,
    ww_hbm,
    wn_hbm,
    lg,
    we_hbm,
    hat_hbm,
    probs_hbm,
    spread_ref,
    keys_ref,
    embedded_ref,
    pooled_ref,
    middle_ref,
    slope_ref,
    hat_rows_ref,
    loss_ref,
    hits_ref,
    scale_ref,
    grad_all_ref,
    late_ref,
    queries_ref,
    back_ref,
    values_ref,
    rows_one_ref,
    rows_mid_ref,
    s_own,
    s_other,
    s_triple,
    s_wo,
    s_ww,
    s_wn,
    s_we,
    s_hat,
    s_probs,
    s_rows,
    s_two,
    s_turn,
    s_slab,
    sems,
    hidden_sems,
):
    pairs, tokens, full_width, full_hidden, stages = dims
    all_pairs = own_rel.shape[0]
    block = block_rows(all_pairs)
    here = lax.axis_index("dp")
    is_text, width, mask = tower_sizes(full_width, full_hidden)
    rows = full_width // HEAD * pairs
    get_we = fetch(we_hbm.at[0], s_we, sems.at[0])
    hidden = Hidden(ww_hbm, wn_hbm, s_ww, s_wn, hidden_sems, full_hidden // CHUNK)
    hidden.start((1, 0))
    get_wo = fetch(wo_hbm.at[0], s_wo, sems.at[1])
    get_triple = fetch(triple_hbm.at[0], s_triple, sems.at[2])
    get_hat = fetch(hat_hbm, s_hat, sems.at[3])
    get_probs = fetch(probs_hbm, s_probs, sems.at[4])

    def place(index):
        at = pl.multiple_of(index * block, block)
        s_own[pl.ds(at, block), :] = in_order([own_rel], stages, pairs, block, at)
        s_other[pl.ds(at, block), :] = in_order([other_rel], stages, pairs, block, at)

    over_blocks(all_pairs // block, place)
    live = (flags_ref[...] > 0).astype(F32)
    live_pairs = jnp.sum(live, axis=1, keepdims=True)
    factor = jnp.exp(logit_scale[...])
    row_weight = loss_scale[...] / (2.0 * live_pairs)
    loss_ref[...] = jnp.zeros_like(loss_ref)
    hits_ref[...] = jnp.zeros_like(hits_ref)
    scale_ref[...] = jnp.zeros_like(scale_ref)
    grad_all_ref[...] = jnp.zeros_like(grad_all_ref)

    def part(index):
        at = pl.multiple_of(index * block, block)
        eye = at + iota((block, all_pairs), 0) == iota((block, all_pairs), 1)
        live_rows = jnp.sum(jnp.where(eye, live, 0.0), axis=1, keepdims=True)

        def one_way(left, right):
            logits = mm_nt(left, right) * factor
            masked = jnp.where(live > 0.5, logits, -1e30)
            peak = jnp.max(masked, axis=1, keepdims=True)
            powers = jnp.exp(masked - peak)
            total = jnp.sum(powers, axis=1, keepdims=True)
            log_total = peak + jnp.log(total)
            matched = jnp.sum(jnp.where(eye, logits, 0.0), axis=1, keepdims=True)
            gap = jnp.where(live_rows > 0.5, log_total - matched, 0.0)
            grads = (
                (powers / total - eye.astype(F32)) * (live_rows * row_weight)
            ).astype(BF16)
            loss = jnp.sum(live_rows * gap, axis=0, keepdims=True)
            hits = jnp.sum(live_rows * jnp.exp(-gap), axis=0, keepdims=True)
            scale = jnp.sum(
                jnp.sum(grads.astype(F32) * logits, axis=1, keepdims=True),
                axis=0,
                keepdims=True,
            )
            return grads, loss, hits, scale

        own = s_own[pl.ds(at, block), :]
        other = s_other[pl.ds(at, block), :]
        grads, loss_one, hits_one, scale_one = one_way(own, s_other[...])
        grad_all_ref[pl.ds(at, block), :] += factor * mm(grads, s_other[...])
        grads, loss_two, hits_two, scale_two = one_way(other, s_own[...])
        grad_all_ref[...] += factor * mm_tn(grads, other)
        loss_ref[...] += loss_one + loss_two
        hits_ref[...] += hits_one + hits_two
        scale_ref[...] += scale_one + scale_two

    over_blocks(all_pairs // block, part)
    loss_ref[...] = loss_ref[...] / (2.0 * live_pairs)
    hits_ref[...] = hits_ref[...] / (2.0 * live_pairs)

    for pair in range(pairs):
        s_rows[pair : pair + 1, :] = grad_all_ref[pl.ds(here * pairs + pair, 1), :]

    gain, shift = ag[...] * mask, ab[...] * mask
    grad_embed = embed_back(embedded_ref[...], s_rows[...])
    get_we.wait()
    grad_three = mm_nt(grad_embed, s_we[...])
    out_hat, out_inv = normed(pooled_ref[...], mask, width)
    grad_pooled = norm_back(out_hat, out_inv, lg[...] * mask, grad_three, mask, width)
    branch = grad_pooled.astype(BF16)
    s_two[...] = jnp.zeros_like(s_two)

    def backward(at):
        grad_active = mm_nt(branch, s_wn[at, :])
        grad_hidden = (grad_active * slope_ref[:, at]).astype(BF16)
        s_two[...] += mm_nt(grad_hidden, s_ww[:, at])

    hidden.each(backward)
    mid_hat, mid_inv = normed(middle_ref[...], mask, width)
    grad_two = s_two[...] * mask
    grad_middle = grad_pooled + norm_back(mid_hat, mid_inv, fg[...] * mask, grad_two, mask, width)
    rows_mid_ref[...] = grad_middle
    attention = grad_middle.astype(BF16)
    get_wo.wait()
    grad_mixed = (mm_nt(attention, s_wo[...]) * mask).astype(BF16)
    repeat = repeat_rows(rows, pairs)
    heads = head_mask(rows, pairs, full_width)
    wide = jnp.where(heads, mm(repeat, grad_mixed), 0.0)
    get_triple.wait()
    along = mm_nt(wide.astype(BF16), s_triple[2])
    values_low = along.astype(BF16)
    values_ref[...] = values_low
    offset = jnp.sum(along * shift, axis=1, keepdims=True) + jnp.sum(
        wide * triple_bias[0, 1:2, :], axis=1, keepdims=True
    )
    get_hat.wait()
    get_probs.wait()
    grad_probs = mm_nt((along * gain).astype(BF16), s_hat[...]) + offset
    probs = s_probs[...]
    inner = jnp.sum(grad_probs * probs, axis=1, keepdims=True)
    back = (probs * (grad_probs - inner)).astype(BF16)
    back_ref[...] = back
    spread = mm(back, s_hat[...])
    total = jnp.sum(back.astype(F32), axis=1, keepdims=True)
    means = (spread * gain + total * shift).astype(BF16)
    query_wide = mm(means, s_triple[1]) * 0.125
    grad_query = mm_tn(repeat, jnp.where(heads, query_wide, 0.0).astype(BF16)).astype(BF16)
    queries_ref[...] = grad_query
    rows_one = mm_nt(grad_query, s_triple[0]) * mask
    rows_one_ref[...] = rows_one
    values_wide = values_low.astype(F32)
    keys_wide = keys_ref[...].astype(F32)
    prob_total = jnp.sum(probs.astype(BF16).astype(F32), axis=1, keepdims=True)
    gain_sum = (
        sums_of(values_wide * spread_ref[...])
        + sums_of(keys_wide * spread)
        + sums_of(rows_one * hat_rows_ref[...].astype(F32))
    ) * mask
    shift_sum = (
        sums_of(values_wide * prob_total) + sums_of(keys_wide * total) + sums_of(rows_one)
    ) * mask
    s_turn[rows:, :] = jnp.zeros((s_turn.shape[0] - rows, full_width), F32)
    s_turn[0:rows, :] = means.astype(F32)
    slot = rows
    for vector in (gain_sum, shift_sum):
        for _ in range(3):
            low = vector.astype(BF16).astype(F32)
            s_turn[slot : slot + 1, :] = low
            vector = vector - low
            slot += 1
    lanes = s_turn.shape[0]
    late_ref[:, 0:lanes] = s_turn[...].T.astype(BF16)
    if late_ref.shape[1] > lanes:
        turned = grad_query.astype(F32).T
        slab = s_slab.shape[0]
        s_slab[...] = jnp.zeros_like(s_slab)
        for place in range(full_width // slab):
            down = slice(place * slab, (place + 1) * slab)
            s_slab[:, place * pairs : (place + 1) * pairs] = turned[down, :]
        slab_low = s_slab[...].astype(BF16)
        for place in range(full_width // slab):
            late_ref[place * slab : (place + 1) * slab, lanes:] = slab_low


def rows_kernel(dims, *refs):
    pairs, tokens, full_width, full_hidden, slice_width, slice_hidden, stages, pieces = dims
    early_hbm = refs[:pieces]
    (
        ends_ref,
        hat_hbm,
        inv_hbm,
        probs_hbm,
        back_ref,
        value_factors_ref,
        keys_ref,
        rows_one_ref,
        rows_mid_ref,
        grad_hbm,
        ag,
        ab,
        triple_hbm,
        triple_bias,
        wo_hbm,
        bo,
        fg,
        fb,
        ww_hbm,
        bw,
        wn_hbm,
        lg,
        lb,
        we_hbm,
        out_hbm,
        ones_ref,
        queries_ref,
        values_ref,
        embed_ref,
        narrow_ref,
        widen_ref,
        mixer_ref,
        final_gain_ref,
        final_bias_ref,
        feed_gain_ref,
        feed_bias_ref,
        narrow_bias_ref,
        mixer_bias_ref,
        value_bias_ref,
        widen_bias_ref,
        s_triple,
        s_wo,
        s_ww,
        s_wn,
        s_we,
        s_vectors,
        s_hat,
        s_inv,
        s_probs,
        s_left,
        s_right,
        s_early,
        grad_ref,
        s_out,
        s_total,
        s_active,
        s_hidden,
        sems,
        hidden_sems,
        out_sems,
    ) = refs[pieces:]
    all_pairs = grad_ref.shape[0]
    block = block_rows(all_pairs)
    here = lax.axis_index("dp")
    is_text, width, mask = tower_sizes(full_width, full_hidden)
    get_probs = fetch(probs_hbm, s_probs, sems.at[3])
    get_hat = fetch(hat_hbm, s_hat, sems.at[4])
    get_inv = fetch(inv_hbm, s_inv, sems.at[5])
    get_grad = fetch(grad_hbm, grad_ref, sems.at[6])
    height = s_early.shape[0] // pieces
    early = [s_early.at[pl.ds(place * height, height), :] for place in range(pieces)]
    get_early = [fetch(early_hbm[place], early[place], sems.at[7 + place]) for place in range(pieces)]
    get_wo = fetch(wo_hbm.at[0], s_wo, sems.at[1])
    get_we = fetch(we_hbm.at[0], s_we, sems.at[2])
    hidden = Hidden(ww_hbm, wn_hbm, s_ww, s_wn, hidden_sems, full_hidden // CHUNK)
    hidden.start((0, 1))
    get_triple = fetch(triple_hbm.at[0, 0], s_triple, sems.at[0])
    rows = full_width // HEAD * pairs
    token_gain = ag[...] * mask
    s_left[rows : 2 * rows, :] = back_ref[...]
    s_right[0:rows, :] = value_factors_ref[...]
    s_right[rows : 2 * rows, :] = keys_ref[...]
    spots = pooled_spots(ends_ref, is_text, pairs, 3)
    s_left[2 * rows :, :] = one_hot(iota((3 * pairs, tokens), 1).astype(F32) == spots)
    s_right[2 * rows :, :] = three_parts(rows_one_ref[...])
    middle_parts = three_parts(rows_mid_ref[...])
    ones = one_hot(iota((full_width, 128), 0).astype(F32) < width)
    get_probs.wait()
    s_left[0:rows, :] = s_probs[...].astype(BF16)
    get_hat.wait()
    get_inv.wait()

    def put(at, count):
        spot = pl.ds(at, count)
        return pltpu.make_async_copy(
            s_out.at[spot, :], out_hbm.at[0, spot, :], out_sems.at[at // NORM_ROWS]
        )

    def norm_rows(at, count):
        spot = pl.ds(at, count)
        upward = mm_tn(s_left[:, spot], s_right[...])
        hat = s_hat[spot, :].astype(F32)
        scaled = upward * token_gain
        mean = mm(scaled.astype(BF16), ones) / width
        along = mm((scaled * hat).astype(BF16), ones) / width
        s_out[spot, :] = across(s_inv[spot, :], full_width) * (
            scaled - (across(mean, full_width) + hat * across(along, full_width)) * mask
        ) + mm_tn(s_left[2 * rows :, spot], middle_parts)
        put(at, count).start()

    over_tokens(tokens, NORM_ROWS, norm_rows)
    for ref in (embed_ref, narrow_ref, widen_ref, mixer_ref, widen_bias_ref, s_vectors):
        ref[...] = jnp.zeros_like(ref)
    lane = iota((full_width, slice_width), 0)
    pick = one_hot(
        (lane == here * slice_width + iota((full_width, slice_width), 1))
        & (lane.astype(F32) < width)
    )
    hidden_width = jnp.where(is_text, MLP_TXT, full_hidden)
    gain, shift = lg[...] * mask, lb[...] * mask
    feed_gain = fg[...] * mask
    get_wo.wait()
    get_we.wait()
    get_grad.wait()
    for copy in get_early:
        copy.wait()

    def part(index):
        at = pl.multiple_of(index * block, block)
        here_rows = pl.ds(at, block)
        arrived = in_order(early, stages, pairs, block, at)
        mixed = arrived[:, 0:full_width]
        stream_rows = arrived[:, full_width : 2 * full_width].astype(F32)
        out_hat = arrived[:, 2 * full_width : 3 * full_width].astype(F32)
        out_inv = jnp.sum(arrived[:, 3 * full_width :].astype(F32), axis=1, keepdims=True)
        three = (out_hat * gain + shift).astype(BF16)
        grad_embed = embed_back(mm(three, s_we[...]), grad_ref[here_rows, :])
        embed_ref[0] += mm_tn(mm(three, pick).astype(BF16), grad_embed)
        grad_three = mm_nt(grad_embed, s_we[...])
        s_vectors[0:1, :] += sums_of(grad_three * out_hat)
        s_vectors[1:2, :] += sums_of(grad_three)
        grad_pooled = norm_back(out_hat, out_inv, gain, grad_three, mask, width)
        branch = grad_pooled.astype(BF16)
        s_vectors[2:3, :] += sums_of(branch.astype(F32))
        middle = stream_rows + mm(mixed, s_wo[...]) + bo[...]
        mid_hat, mid_inv = normed(middle, mask, width)
        two = ((mid_hat * fg[...] + fb[...]) * mask).astype(BF16)
        s_total[...] = jnp.zeros_like(s_total)
        s_active[...] = jnp.zeros_like(s_active)
        s_hidden[...] = jnp.zeros_like(s_hidden)

        def through(chunk, carry):
            first = pl.multiple_of(chunk * CHUNK, CHUNK)
            lanes = pl.ds(first, CHUNK)
            if all_pairs == block:
                hidden.wait(chunk)
            pre = mm(two, s_ww[:, lanes]) + bw[:, lanes]
            gate = sigmoid(1.702 * pre)
            active = pre * gate
            there = (first + iota((1, CHUNK), 1) < hidden_width).astype(F32)
            slope = (gate + 1.702 * active * (1.0 - gate)) * there
            grad_hidden = (mm_nt(branch, s_wn[lanes, :]) * slope).astype(BF16)
            s_total[...] += mm_nt(grad_hidden, s_ww[:, lanes])
            row = first + iota((CHUNK, slice_hidden), 0)
            chosen = one_hot(
                (row == here * slice_hidden + iota((CHUNK, slice_hidden), 1))
                & (row < hidden_width)
            )
            s_active[...] += mm(active.astype(BF16), chosen)
            s_hidden[...] += mm(grad_hidden, chosen)
            return carry

        lax.fori_loop(0, full_hidden // CHUNK, through, 0)
        grad_two, active_slice, hidden_slice = s_total[...], s_active[...], s_hidden[...]
        narrow_ref[0] += mm_tn(active_slice.astype(BF16), branch)
        widen_ref[0] += mm_tn(hidden_slice.astype(BF16), two)
        widen_bias_ref[...] += sums_of(hidden_slice)
        s_vectors[3:4, :] += sums_of(grad_two * mid_hat)
        s_vectors[4:5, :] += sums_of(grad_two)
        grad_middle = grad_pooled + norm_back(mid_hat, mid_inv, feed_gain, grad_two, mask, width)
        attention = grad_middle.astype(BF16)
        s_vectors[5:6, :] += sums_of(attention.astype(F32))
        mixer_ref[0] += mm_tn(mm(mixed, pick).astype(BF16), attention)
        grad_mixed = (mm_nt(attention, s_wo[...]) * mask).astype(BF16)
        values_ref[here_rows, :] = grad_mixed
        s_vectors[6:7, :] += sums_of(grad_mixed.astype(F32))
        rows_hat, _ = normed(stream_rows, mask, width)
        one = ((rows_hat * ag[...] + ab[...]) * mask).astype(BF16)
        ones_ref[here_rows, :] = mm(one, pick).astype(BF16)
        if all_pairs == block:
            get_triple.wait()
        query = (mm(one, s_triple[...]) + triple_bias[0, 0:1, :]) * mask
        queries_ref[here_rows, :] = query.astype(BF16)

    if all_pairs != block:
        get_triple.wait()
        for chunk in range(full_hidden // CHUNK):
            hidden.wait(chunk)
    over_blocks(all_pairs // block, part)
    over_tokens(tokens, NORM_ROWS, lambda at, count: put(at, count).wait())
    vectors = dot_dims(s_vectors[...], pick.astype(F32), 1, 0, lax.Precision.HIGHEST)
    for slot, ref in enumerate(
        (
            final_gain_ref,
            final_bias_ref,
            narrow_bias_ref,
            feed_gain_ref,
            feed_bias_ref,
            mixer_bias_ref,
            value_bias_ref,
        )
    ):
        ref[...] = vectors[slot : slot + 1, :]


def last_kernel(dims, *refs):
    pairs, full_width, full_hidden, slice_width, stages, pieces = dims
    arrived = refs[:pieces]
    (
        late_ref,
        means_ref,
        ones_ref,
        queries_ref,
        values_ref,
        value_bias_ref,
        triple_ref,
        gain_ref,
        shift_ref,
        bias_ref,
        s_keys,
        s_means,
        s_turned,
        s_late,
        s_sums,
    ) = refs[pieces:]
    here = lax.axis_index("dp")
    count = late_ref.shape[0]
    lanes = means_ref.shape[2]
    heads = full_width // HEAD
    rows = heads * pairs
    all_pairs = queries_ref.shape[0]
    s_late[...] = jnp.zeros_like(s_late)
    if not arrived:
        for source in range(count):
            now = late_ref[source]
            s_late[...] += now[:, 0:lanes].astype(F32)
            means = means_ref[source]
            across_now = slice(source * pairs, (source + 1) * pairs)
            for head in range(heads):
                down = slice(head * slice_width, (head + 1) * slice_width)
                lane = slice(head * pairs, (head + 1) * pairs)
                s_keys[down, across_now] = now[:, lane]
                s_means[down, across_now] = means[:, lane]
            for slab in range(count):
                down = slice(slab * slice_width, (slab + 1) * slice_width)
                first = lanes + slab * pairs
                s_turned[down, across_now] = now[:, first : first + pairs]
        left = iota((slice_width, 2 * HEAD), 1) < HEAD
        for two in range(heads // 2):
            down = slice(two * 2 * slice_width, (two + 1) * 2 * slice_width)
            lane = slice(two * 2 * HEAD, (two + 1) * 2 * HEAD)
            both = mm(s_keys[down, :], queries_ref[:, lane]) * 0.125
            triple_ref[0, 1, :, lane] = jnp.where(left, both[0:slice_width], both[slice_width:])
            both = mm(s_means[down, :], values_ref[:, lane])
            triple_ref[0, 2, :, lane] = jnp.where(left, both[0:slice_width], both[slice_width:])
        triple_ref[0, 0] = mm(s_turned[...], ones_ref[...]).T
        mine = s_turned[pl.ds(pl.multiple_of(here * slice_width, slice_width), slice_width), :]
        sums = mm_nt(jnp.ones((8, all_pairs), BF16), mine)
    else:
        block = block_rows(all_pairs)
        triple_ref[...] = jnp.zeros_like(triple_ref)
        s_sums[...] = jnp.zeros_like(s_sums)

        def part(index):
            at = pl.multiple_of(index * block, block)
            grad_query = in_order(arrived, stages, pairs, block, at)
            triple_ref[0, 0] += mm_tn(ones_ref[pl.ds(at, block), :], grad_query)
            s_sums[0:1, :] += sums_of(grad_query.astype(F32))

        over_blocks(all_pairs // block, part)
        head = head_mask(lanes, pairs, full_width)

        def one(source, carry):
            now = late_ref[source]
            s_late[...] += now.astype(F32)
            row = iota((lanes, all_pairs), 0)
            column = iota((lanes, all_pairs), 1)
            repeat = one_hot((column == source * pairs + lax.rem(row, pairs)) & (row < rows))
            means = means_ref[source]
            for which, left, origin in ((1, now, queries_ref), (2, means, values_ref)):
                wide = jnp.where(head, mm(repeat, origin[...]), 0.0).astype(BF16)
                triple_ref[0, which] += mm(left, wide)
            return carry

        lax.fori_loop(0, count, one, 0)
        triple_ref[0, 1] = triple_ref[0, 1] * 0.125
        pick = (
            iota((full_width, slice_width), 0)
            == here * slice_width + iota((full_width, slice_width), 1)
        ).astype(F32)
        sums = dot_dims(s_sums[...], pick, 1, 0, lax.Precision.HIGHEST)
    lane = iota((8, lanes), 1)
    row = iota((8, lanes), 0)
    slot = rows + row * 3
    chosen = ((lane >= slot) & (lane < slot + 3) & (row < 2)).astype(F32)
    from_late = dot_dims(chosen, s_late[...], 1, 1, lax.Precision.HIGHEST)
    gain_ref[...] = from_late[0:1, :]
    shift_ref[...] = from_late[1:2, :]
    bias_ref[0, 0:1, :] = sums[0:1, :]
    bias_ref[0, 1:2, :] = value_bias_ref[...]


def stages_of(count):
    bits = count.bit_length() - 1
    stages = []
    while bits > 0:
        take = 2 if bits >= 2 else 1
        bits -= take
        stages.append((bits, take))
    return tuple(stages)


def exchange(block, axis, stage):
    count = lax.axis_size(axis)
    shift, bits = stage
    parts = [block]
    for apart in range(1, 1 << bits):
        route = [(low, low ^ (apart << shift)) for low in range(count)]
        parts.append(lax.ppermute(block, axis, route))
    return parts


def call(
    kernel, ins, outs, scratch, in_hbm=(), out_hbm=(), cost=None, kept=(), limit=VMEM_LIMIT
):
    vmem = pl.BlockSpec(memory_space=pltpu.VMEM)
    anywhere = pl.BlockSpec(memory_space=pl.ANY)
    specs = [anywhere if index in in_hbm else vmem for index in range(len(ins))]
    out_specs = [anywhere if index in out_hbm else vmem for index in range(len(outs))]
    if kept:
        ins = [
            pltpu.with_memory_space_constraint(
                array, pltpu.VMEM if index in kept else pltpu.HBM
            )
            for index, array in enumerate(ins)
        ]
    flops, moved = cost
    return pl.pallas_call(
        kernel,
        out_shape=[jax.ShapeDtypeStruct(shape, kind) for shape, kind in outs],
        in_specs=specs,
        out_specs=out_specs,
        scratch_shapes=scratch,
        compiler_params=pltpu.CompilerParams(vmem_limit_bytes=limit),
        cost_estimate=pl.CostEstimate(flops=flops, bytes_accessed=moved, transcendentals=0),
    )(*ins)


def body(
    block_input,
    segments,
    caption_ends,
    pair_flags,
    attention_gain,
    attention_bias,
    triple_weight,
    triple_bias,
    mixer_weight,
    mixer_bias,
    feed_gain,
    feed_bias,
    widen_weight,
    widen_bias,
    narrow_weight,
    narrow_bias,
    final_gain,
    final_bias,
    embed_weight,
    logit_scale,
    loss_scale,
):
    tokens, width = block_input.shape[1:]
    hidden = widen_weight.shape[2]
    emb = embed_weight.shape[2]
    pairs = caption_ends.shape[0]
    count = lax.axis_size("dp")
    all_pairs = pair_flags.shape[0]
    heads = width // HEAD
    rows = heads * pairs
    lanes = -(-(rows + 12) // 128) * 128
    slice_width = width // count
    slice_hidden = hidden // count
    stages = stages_of(count)
    compact = count <= 16 and slice_width % 16 == 0
    slab_lanes = -(-all_pairs // 128) * 128
    ends = caption_ends.reshape(1, pairs)
    dma = pltpu.SemaphoreType.DMA
    weights_scratch = [
        pltpu.VMEM((3, width, width), BF16),
        pltpu.VMEM((width, width), BF16),
        pltpu.VMEM((width, hidden), BF16),
        pltpu.VMEM((hidden, width), BF16),
        pltpu.VMEM((width, emb), BF16),
    ]
    dims = (pairs, tokens, width, hidden)
    chunk_count = hidden // CHUNK
    (
        unit,
        early,
        hat,
        invert,
        probs,
        query,
        embedded,
        pooled,
        middle,
        slope,
    ) = call(
        partial(attend_kernel, dims),
        (
            ends,
            block_input,
            attention_gain,
            attention_bias,
            triple_weight,
            triple_bias,
            mixer_weight,
            mixer_bias,
            feed_gain,
            feed_bias,
            widen_weight,
            widen_bias,
            narrow_weight,
            narrow_bias,
            final_gain,
            final_bias,
            embed_weight,
        ),
        [
            ((pairs, emb), BF16),
            ((pairs, 3 * width + 128), BF16),
            ((tokens, width), BF16),
            ((tokens, 128), F32),
            ((rows, tokens), F32),
            ((pairs, width), BF16),
            ((pairs, emb), F32),
            ((pairs, width), F32),
            ((pairs, width), F32),
            ((pairs, hidden), F32),
        ],
        [
            pltpu.VMEM((tokens, width), BF16),
            pltpu.VMEM((tokens, width), BF16),
            pltpu.VMEM((tokens, width), BF16),
            pltpu.VMEM((tokens, 128), F32),
            pltpu.VMEM((rows, tokens), F32),
            pltpu.VMEM((tokens, width), BF16),
            pltpu.VMEM((tokens, width), BF16),
        ]
        + weights_scratch
        + [
            pltpu.VMEM((rows, tokens), BF16),
            dma((7,)),
            dma((2, chunk_count)),
        ],
        in_hbm=(1, 4, 6, 10, 12, 16),
        out_hbm=(2, 3, 4),
        cost=(10**9, 20 * 10**6),
    )
    turned, spread, keys, hat_rows = call(
        partial(means_kernel, dims),
        (ends, attention_gain, attention_bias, hat, probs, query, triple_weight),
        [
            ((width, lanes), BF16),
            ((rows, width), F32),
            ((rows, width), BF16),
            ((pairs, width), BF16),
        ],
        [
            pltpu.VMEM((width, width), BF16),
            pltpu.VMEM((lanes, width), F32),
            dma((1,)),
        ],
        in_hbm=(6,),
        cost=(10**9, 5 * 10**6),
    )
    early_rows, own_rel = early, unit
    flags = pair_flags.reshape(1, all_pairs)
    for index, stage in enumerate(stages):
        own_parts = exchange(own_rel, "dp", stage)
        if index + 1 < len(stages):
            own_parts, early_rows, turned, spread, keys, hat_rows, flags = lax.optimization_barrier(
                (own_parts, early_rows, turned, spread, keys, hat_rows, flags)
            )
            early_rows = jnp.concatenate(exchange(early_rows, "dp", stage), axis=0)
        own_rel = jnp.concatenate(own_parts, axis=0)
    means_all = lax.all_to_all(turned, "dp", 0, 0, tiled=True).reshape(count, slice_width, lanes)
    other_rel = lax.ppermute(own_rel, "tower", [(0, 1), (1, 0)])
    early_pieces = exchange(early_rows, "dp", stages[-1])
    (
        loss,
        hits,
        scale,
        grad_all,
        late,
        queries,
        back,
        values,
        rows_one,
        rows_mid,
    ) = call(
        partial(loss_kernel, dims + (stages,)),
        (
            own_rel,
            other_rel,
            flags,
            logit_scale.reshape(1, 1),
            loss_scale.reshape(1, 1),
            attention_gain,
            attention_bias,
            triple_weight,
            triple_bias,
            mixer_weight,
            feed_gain,
            widen_weight,
            narrow_weight,
            final_gain,
            embed_weight,
            hat,
            probs,
            spread,
            keys,
            embedded,
            pooled,
            middle,
            slope,
            hat_rows,
        ),
        [
            ((1, 1), F32),
            ((1, 1), F32),
            ((1, 1), F32),
            ((all_pairs, emb), F32),
            ((width, lanes + (slab_lanes if compact else 0)), BF16),
            ((pairs, width), BF16),
            ((rows, tokens), BF16),
            ((rows, width), BF16),
            ((pairs, width), F32),
            ((pairs, width), F32),
        ],
        [pltpu.VMEM((all_pairs, emb), BF16), pltpu.VMEM((all_pairs, emb), BF16)]
        + weights_scratch
        + [
            pltpu.VMEM((tokens, width), BF16),
            pltpu.VMEM((rows, tokens), F32),
            pltpu.VMEM((pairs, emb), F32),
            pltpu.VMEM((pairs, width), F32),
            pltpu.VMEM((lanes, width), F32),
            pltpu.VMEM((slice_width, slab_lanes), F32),
            dma((5,)),
            dma((2, chunk_count)),
        ],
        in_hbm=(7, 9, 11, 12, 14, 15, 16),
        cost=(10**9, 20 * 10**6),
    )
    early_pieces, late, queries = lax.optimization_barrier((early_pieces, late, queries))
    late_all = lax.all_to_all(late, "dp", 0, 0, tiled=True)
    late_all = late_all.reshape(count, slice_width, late.shape[1])
    late_pieces = []
    if not compact:
        late_pieces = [queries]
        for stage in stages:
            late_pieces = exchange(jnp.concatenate(late_pieces, axis=0), "dp", stage)
    ahead = len(early_pieces)
    vector = ((1, slice_width), F32)
    (
        block_grad,
        ones,
        query_rows,
        value_rows,
        grad_embed,
        grad_narrow,
        grad_widen,
        grad_mixer,
        grad_final_gain,
        grad_final_bias,
        grad_feed_gain,
        grad_feed_bias,
        grad_narrow_bias,
        grad_mixer_bias,
        grad_value_bias,
        grad_widen_bias,
    ) = call(
        partial(
            rows_kernel,
            (pairs, tokens, width, hidden, slice_width, slice_hidden, stages, ahead),
        ),
        tuple(early_pieces)
        + (
            ends,
            hat,
            invert,
            probs,
            back,
            values,
            keys,
            rows_one,
            rows_mid,
            grad_all,
            attention_gain,
            attention_bias,
            triple_weight,
            triple_bias,
            mixer_weight,
            mixer_bias,
            feed_gain,
            feed_bias,
            widen_weight,
            widen_bias,
            narrow_weight,
            final_gain,
            final_bias,
            embed_weight,
        ),
        [
            ((1, tokens, width), F32),
            ((all_pairs, slice_width), BF16),
            ((all_pairs, width), BF16),
            ((all_pairs, width), BF16),
            ((1, slice_width, emb), F32),
            ((1, slice_hidden, width), F32),
            ((1, slice_hidden, width), F32),
            ((1, slice_width, width), F32),
        ]
        + [vector] * 7
        + [((1, slice_hidden), F32)],
        [pltpu.VMEM((width, width), BF16)]
        + weights_scratch[1:]
        + [
            pltpu.VMEM((8, width), F32),
            pltpu.VMEM((tokens, width), BF16),
            pltpu.VMEM((tokens, 128), F32),
            pltpu.VMEM((rows, tokens), F32),
            pltpu.VMEM((2 * rows + 3 * pairs, tokens), BF16),
            pltpu.VMEM((2 * rows + 3 * pairs, width), BF16),
            pltpu.VMEM((all_pairs, 3 * width + 128), BF16),
            pltpu.VMEM((all_pairs, emb), F32),
            pltpu.VMEM((tokens, width), F32),
            pltpu.VMEM((block_rows(all_pairs), width), F32),
            pltpu.VMEM((block_rows(all_pairs), slice_hidden), F32),
            pltpu.VMEM((block_rows(all_pairs), slice_hidden), F32),
            dma((7 + ahead,)),
            dma((2, chunk_count)),
            dma((-(-tokens // NORM_ROWS),)),
        ],
        in_hbm=tuple(range(ahead)) + tuple(ahead + index for index in (1, 2, 3, 9, 12, 14, 18, 20, 23)),
        out_hbm=(0,),
        cost=(3 * 10**9, 10 * 10**6),
    )
    grad_triple, grad_gain, grad_bias, grad_triple_bias = call(
        partial(last_kernel, (pairs, width, hidden, slice_width, stages, len(late_pieces))),
        tuple(late_pieces)
        + (late_all, means_all, ones, query_rows, value_rows, grad_value_bias),
        [
            ((1, 3, slice_width, width), F32),
            vector,
            vector,
            ((1, 2, slice_width), F32),
        ],
        [
            pltpu.VMEM((width // HEAD * slice_width, all_pairs), BF16),
            pltpu.VMEM((width // HEAD * slice_width, all_pairs), BF16),
            pltpu.VMEM((width, all_pairs), BF16),
            pltpu.VMEM((slice_width, lanes), F32),
            pltpu.VMEM((8, width), F32),
        ],
        cost=(10**9, 10 * 10**6),
        kept=(0,) if compact else (),
        limit=32 * 1024 * 1024 if compact else VMEM_LIMIT,
    )
    return (
        loss[0, 0],
        hits[0, 0],
        block_grad,
        grad_gain,
        grad_bias,
        grad_triple,
        grad_triple_bias,
        grad_mixer,
        grad_mixer_bias,
        grad_feed_gain,
        grad_feed_bias,
        jnp.swapaxes(grad_widen, 1, 2),
        grad_widen_bias,
        grad_narrow,
        grad_narrow_bias,
        grad_final_gain,
        grad_final_bias,
        grad_embed,
        scale[0, 0],
    )


def solution(mesh):
    in_specs = (
        P("tower", "dp", None),
        P("dp", None),
        P("dp"),
        P(),
        P("tower", None),
        P("tower", None),
        P("tower", None, None, None),
        P("tower", None, None),
        P("tower", None, None),
        P("tower", None),
        P("tower", None),
        P("tower", None),
        P("tower", None, None),
        P("tower", None),
        P("tower", None, None),
        P("tower", None),
        P("tower", None),
        P("tower", None),
        P("tower", None, None),
        P(),
        P(),
    )
    out_specs = (
        P(),
        P(),
        P("tower", "dp", None),
        P("tower", "dp"),
        P("tower", "dp"),
        P("tower", None, "dp", None),
        P("tower", None, "dp"),
        P("tower", "dp", None),
        P("tower", "dp"),
        P("tower", "dp"),
        P("tower", "dp"),
        P("tower", None, "dp"),
        P("tower", "dp"),
        P("tower", "dp", None),
        P("tower", "dp"),
        P("tower", "dp"),
        P("tower", "dp"),
        P("tower", "dp", None),
        P(),
    )
    return jax.shard_map(body, mesh=mesh, in_specs=in_specs, out_specs=out_specs, check_vma=False)
```

profile of v0, /device:TPU:0, one launch (start us, length us, event | category | flops | bytes accessed | tf_op | source)
XLA Modules:
  0.0 99.0 jit_solution(17012959956925017149)
XLA Ops:
  0.7 13.9 %shard_map.339 = (bf16[20,512]{1,0:T(8,128)(2,1)}, bf16[20,2432]{1,0:T(8,128)(2,1)}, bf16[1080,768]{1,0:T(8,128)(2,1)}, f32[1080,128]{1,0:T(8,128)}, f32[240,108...) custom-call(s32[1,20]{1,0:T(1,128)} %bitcast.13, ...), custom_call_target="tpu_custom_call" | custom-call | flops 1000000000 | bytes 20000000 | tf_op jit(solution)/shard_map/pallas_call | solution.py:944
  14.5 0.0 copy-start.7
  14.5 0.0 copy-start.6
  14.6 0.0 copy-start.5
  14.6 5.1 %collective-permute-start.2 = (bf16[20,512]{1,0:T(8,128)(2,1)}, bf16[20,512]{1,0:T(8,128)(2,1)S(1)}, u32[]{:S(2)}, u32[]{:S(2)}) collective-permute-start(bf16[20,512]{1,0:T(8,128)(2,1)} %get-tuple-element.86), channel_id=1, source_target_pairs={{0,12},{1,13},{2,14},{3,15},{4,8},{5,9},{6,10},{7,11},{8,4},{9,5},... | collective-permute-start | bytes 61448 | tf_op jit(solution)/shard_map/ppermute | solution.py:925
  19.7 0.0 collective-permute-start.1
  19.7 0.6 collective-permute-start
  20.3 4.4 %shard_map.340 = (bf16[768,256]{1,0:T(8,128)(2,1)}, f32[240,768]{1,0:T(8,128)}, bf16[240,768]{1,0:T(8,128)(2,1)}, bf16[20,768]{1,0:T(8,128)(2,1)}) custom-call(s32[1,20]{1,0:T(1,128)} %bitcast.14, f32[1,768]{1,0:T(1,128)} %refs_14_.1, f32[1,768]{1,0:T(1,128)} %refs_15_.1, bf16[1080,768]{1,0:T(8,128)(2,1)} %get-tuple-element.79.hat_ref.hat_hbm.refs_5_, ...), custom_call_target="tpu_custom_call" | custom-call | flops 1000000000 | bytes 5000000 | tf_op jit(solution)/shard_map/pallas_call | solution.py:944
  24.8 0.0 copy-done.7
  24.8 0.5 reshape.59.flags_ref
  25.3 0.0 collective-permute-done.2
  25.3 0.0 collective-permute-done.1
  25.3 0.0 collective-permute-done
  25.3 0.0 copy-done.6
  25.4 2.7 %collective-permute-start.5 = (bf16[80,512]{1,0:T(8,128)(2,1)S(1)}, bf16[80,512]{1,0:T(8,128)(2,1)S(1)}, u32[]{:S(2)}, u32[]{:S(2)}) collective-permute-start(bf16[80,512]{1,0:T(8,128)(2,1)S(1)} %pad_maximum_fusion.1), channel_id=1, source_target_pairs={{0,3},{1,2},{2,1},{3,0},{4,7},{5,6},{6,5},{7,4},{8,11},{9,10},{10,... | collective-permute-start | bytes 245768 | tf_op jit(solution)/shard_map/ppermute | solution.py:925
  28.0 3.6 %collective-permute-start.9 = (bf16[20,2432]{1,0:T(8,128)(2,1)S(1)}, bf16[20,2432]{1,0:T(8,128)(2,1)S(1)}, u32[]{:S(2)}, u32[]{:S(2)}) collective-permute-start(bf16[20,2432]{1,0:T(8,128)(2,1)S(1)} %copy-done.5), channel_id=1, source_target_pairs={{0,12},{1,13},{2,14},{3,15},{4,8},{5,9},{6,10},{7,11},{8,4},{9,5},... | collective-permute-start | bytes 291848 | tf_op jit(solution)/shard_map/ppermute | solution.py:925
  31.6 0.0 collective-permute-start.8
  31.6 0.8 collective-permute-start.7
  32.4 0.5 collective-permute-start.4
  32.9 0.0 collective-permute-done.5
  32.9 0.4 collective-permute-start.3
  33.3 7.0 %all-to-all-start.1 = ((bf16[16,48,256]{2,1,0:T(8,128)(2,1)}), bf16[16,48,256]{2,1,0:T(8,128)(2,1)S(1)}, u32[]{:S(2)}, u32[]{:S(2)}) async-start(bf16[16,48,256]{2,1,0:T(8,128)(2,1)} %bitcast.12), calls=%async_computation.1 | async-start | bytes 786432 | tf_op jit(solution)/shard_map/all_to_all | solution.py:1093
  40.3 0.0 collective-permute-done.4
  40.3 0.0 collective-permute-done.3
  40.3 0.3 concatenate.11.own_rel
  40.7 0.0 copy-start.1
  40.7 0.1 collective-permute-start.6
  40.8 0.0 collective-permute-done.9
  40.8 0.0 collective-permute-done.8
  40.8 0.0 collective-permute-done.7
  40.8 0.1 pad_maximum_fusion.refs_0_
  40.9 0.0 copy-start
  40.9 2.9 %collective-permute-start.12 = (bf16[80,2432]{1,0:T(8,128)(2,1)S(1)}, bf16[80,2432]{1,0:T(8,128)(2,1)S(1)}, u32[]{:S(2)}, u32[]{:S(2)}) collective-permute-start(bf16[80,2432]{1,0:T(8,128)(2,1)S(1)} %pad_maximum_fusion.refs_0_), channel_id=1, source_target_pairs={{0,3},{1,2},{2,1},{3,0},{4,7},{5,6},{6,5},{7,4},{8,11},{9,10},{10,... | collective-permute-start | bytes 1167368 | tf_op jit(solution)/shard_map/ppermute | solution.py:925
  43.8 0.6 collective-permute-start.11
  44.4 0.1 collective-permute-start.10
  45.8 0.0 collective-permute-done.6.other_rel
  45.8 0.0 copy-start.4
  45.8 0.7 copy-done.4
  46.5 15.6 %shard_map.341 = (f32[1,1]{1,0:T(1,128)}, f32[1,1]{1,0:T(1,128)}, f32[1,1]{1,0:T(1,128)}, f32[320,512]{1,0:T(8,128)}, bf16[768,640]{1,0:T(8,128)(2,1)}, /*index=...) custom-call(bf16[320,512]{1,0:T(8,128)(2,1)} %copy-done.1, ...), custom_call_target="tpu_custom_call" | custom-call | flops 1000000000 | bytes 20000000 | tf_op jit(solution)/shard_map/pallas_call | solution.py:944
  62.1 0.0 collective-permute-done.12.refs_3_
  62.1 2.0 %collective-permute-done.11.refs_2_ = bf16[80,2432]{1,0:T(8,128)(2,1)} collective-permute-done((bf16[80,2432]{1,0:T(8,128)(2,1)S(1)}, bf16[80,2432]{1,0:T(8,128)(2,1)}, u32[]{:S(2)}, u32[]{:S(2)}) %collective-permute-start.11) | collective-permute-done | bytes 389152 | tf_op jit(solution)/shard_map/ppermute | solution.py:925
  64.1 0.0 collective-permute-done.10.refs_1_
  64.1 0.0 all-to-all-done.1.refs_1_
  64.1 5.3 %all-to-all-start = ((bf16[16,48,640]{2,1,0:T(8,128)(2,1)}), bf16[16,48,640]{2,1,0:T(8,128)(2,1)S(1)}, u32[]{:S(2)}, u32[]{:S(2)}) async-start(bf16[16,48,640]{2,1,0:T(8,128)(2,1)} %bitcast.11), calls=%async_computation | async-start | bytes 1966080 | tf_op jit(solution)/shard_map/all_to_all | solution.py:1163
  69.5 22.5 %shard_map.342 = (f32[1,1080,768]{2,1,0:T(8,128)}, bf16[320,48]{1,0:T(8,128)(2,1)}, bf16[320,768]{1,0:T(8,128)(2,1)}, bf16[320,768]{1,0:T(8,128)(2,1)}, f32[1,48...) custom-call(bf16[80,2432]{1,0:T(8,128)(2,1)} %copy-done, ...), custom_call_target="tpu_custom_call" | custom-call | flops 3000000000 | bytes 10000000 | tf_op jit(solution)/shard_map/pallas_call | solution.py:944
  92.0 0.0 copy-done.2
  92.0 0.7 all-to-all-done.refs_0_
  92.7 6.4 %shard_map.343 = (f32[1,3,48,768]{3,2,1,0:T(8,128)}, f32[1,48]{1,0:T(1,128)}, f32[1,48]{1,0:T(1,128)}, f32[1,2,48]{2,1,0:T(2,128)}) custom-call(bf16[16,48,640]{2,1,0:T(8,128)(2,1)S(1)} %all-to-all-done.refs_0_, bf16[16,48,256]{2,1,0:T(8,128)(2,1)} %copy-done.2, bf16[320,48]{1,0:T(8,128)(2,1)} %get-tuple-element.115.refs_2_, ...), custom_call_target="tpu_custom_call" | custom-call | flops 1000000000 | bytes 10000000 | tf_op jit(solution)/shard_map/pallas_call | solution.py:944
  (7 shorter events, 0.0 us)
Async XLA Ops:
  14.5 10.2 %copy-start.7 = (s32[320]{0:T(512)S(1)}, s32[320]{0:T(512)}, u32[]{:S(2)}) copy-start(s32[320]{0:T(512)} %param.23) | copy-start | bytes 3844
  14.5 10.8 %copy-start.6 = (bf16[20,512]{1,0:T(8,128)(2,1)S(1)}, bf16[20,512]{1,0:T(8,128)(2,1)}, u32[]{:S(2)}) copy-start(bf16[20,512]{1,0:T(8,128)(2,1)} %get-tuple-element.86) | copy-start | bytes 61444
  14.6 13.5 %copy-start.5 = (bf16[20,2432]{1,0:T(8,128)(2,1)S(1)}, bf16[20,2432]{1,0:T(8,128)(2,1)}, u32[]{:S(2)}) copy-start(bf16[20,2432]{1,0:T(8,128)(2,1)} %get-tuple-element.100) | copy-start | bytes 291844
  14.6 10.7 %collective-permute-start.2 = (bf16[20,512]{1,0:T(8,128)(2,1)}, bf16[20,512]{1,0:T(8,128)(2,1)S(1)}, u32[]{:S(2)}, u32[]{:S(2)}) collective-permute-start(bf16[20,512]{1,0:T(8,128)(2,1)} %get-tuple-element.86), channel_id=1, source_target_pairs={{0,12},{1,13},{2,14},{3,15},{4,8},{5,9},{6,10},{7,11},{8,4},{9,5},... | collective-permute-start | bytes 61448 | tf_op jit(solution)/shard_map/ppermute | solution.py:925
  19.7 5.6 %collective-permute-start.1 = (bf16[20,512]{1,0:T(8,128)(2,1)}, bf16[20,512]{1,0:T(8,128)(2,1)S(1)}, u32[]{:S(2)}, u32[]{:S(2)}) collective-permute-start(bf16[20,512]{1,0:T(8,128)(2,1)} %get-tuple-element.86), channel_id=1, source_target_pairs={{0,8},{1,9},{2,10},{3,11},{4,12},{5,13},{6,14},{7,15},{8,0},{9,1},... | collective-permute-start | bytes 61448 | tf_op jit(solution)/shard_map/ppermute | solution.py:925
  19.7 5.6 %collective-permute-start = (bf16[20,512]{1,0:T(8,128)(2,1)}, bf16[20,512]{1,0:T(8,128)(2,1)S(1)}, u32[]{:S(2)}, u32[]{:S(2)}) collective-permute-start(bf16[20,512]{1,0:T(8,128)(2,1)} %get-tuple-element.86), channel_id=1, source_target_pairs={{0,4},{1,5},{2,6},{3,7},{4,0},{5,1},{6,2},{7,3},{8,12},{9,13},{10,... | collective-permute-start | bytes 61448 | tf_op jit(solution)/shard_map/ppermute | solution.py:925
  25.4 7.6 %collective-permute-start.5 = (bf16[80,512]{1,0:T(8,128)(2,1)S(1)}, bf16[80,512]{1,0:T(8,128)(2,1)S(1)}, u32[]{:S(2)}, u32[]{:S(2)}) collective-permute-start(bf16[80,512]{1,0:T(8,128)(2,1)S(1)} %pad_maximum_fusion.1), channel_id=1, source_target_pairs={{0,3},{1,2},{2,1},{3,0},{4,7},{5,6},{6,5},{7,4},{8,11},{9,10},{10,... | collective-permute-start | bytes 245768 | tf_op jit(solution)/shard_map/ppermute | solution.py:925
  28.0 12.8 %collective-permute-start.9 = (bf16[20,2432]{1,0:T(8,128)(2,1)S(1)}, bf16[20,2432]{1,0:T(8,128)(2,1)S(1)}, u32[]{:S(2)}, u32[]{:S(2)}) collective-permute-start(bf16[20,2432]{1,0:T(8,128)(2,1)S(1)} %copy-done.5), channel_id=1, source_target_pairs={{0,12},{1,13},{2,14},{3,15},{4,8},{5,9},{6,10},{7,11},{8,4},{9,5},... | collective-permute-start | bytes 291848 | tf_op jit(solution)/shard_map/ppermute | solution.py:925
  31.6 9.2 %collective-permute-start.8 = (bf16[20,2432]{1,0:T(8,128)(2,1)S(1)}, bf16[20,2432]{1,0:T(8,128)(2,1)S(1)}, u32[]{:S(2)}, u32[]{:S(2)}) collective-permute-start(bf16[20,2432]{1,0:T(8,128)(2,1)S(1)} %copy-done.5), channel_id=1, source_target_pairs={{0,8},{1,9},{2,10},{3,11},{4,12},{5,13},{6,14},{7,15},{8,0},{9,1},... | collective-permute-start | bytes 291848 | tf_op jit(solution)/shard_map/ppermute | solution.py:925
  31.6 9.2 %collective-permute-start.7 = (bf16[20,2432]{1,0:T(8,128)(2,1)S(1)}, bf16[20,2432]{1,0:T(8,128)(2,1)S(1)}, u32[]{:S(2)}, u32[]{:S(2)}) collective-permute-start(bf16[20,2432]{1,0:T(8,128)(2,1)S(1)} %copy-done.5), channel_id=1, source_target_pairs={{0,4},{1,5},{2,6},{3,7},{4,0},{5,1},{6,2},{7,3},{8,12},{9,13},{10,... | collective-permute-start | bytes 291848 | tf_op jit(solution)/shard_map/ppermute | solution.py:925
  32.4 7.9 %collective-permute-start.4 = (bf16[80,512]{1,0:T(8,128)(2,1)S(1)}, bf16[80,512]{1,0:T(8,128)(2,1)S(1)}, u32[]{:S(2)}, u32[]{:S(2)}) collective-permute-start(bf16[80,512]{1,0:T(8,128)(2,1)S(1)} %pad_maximum_fusion.1), channel_id=1, source_target_pairs={{0,2},{1,3},{2,0},{3,1},{4,6},{5,7},{6,4},{7,5},{8,10},{9,11},{10,... | collective-permute-start | bytes 245768 | tf_op jit(solution)/shard_map/ppermute | solution.py:925
  32.9 7.4 %collective-permute-start.3 = (bf16[80,512]{1,0:T(8,128)(2,1)S(1)}, bf16[80,512]{1,0:T(8,128)(2,1)S(1)}, u32[]{:S(2)}, u32[]{:S(2)}) collective-permute-start(bf16[80,512]{1,0:T(8,128)(2,1)S(1)} %pad_maximum_fusion.1), channel_id=1, source_target_pairs={{0,1},{1,0},{2,3},{3,2},{4,5},{5,4},{6,7},{7,6},{8,9},{9,8},{10,11... | collective-permute-start | bytes 245768 | tf_op jit(solution)/shard_map/ppermute | solution.py:925
  33.3 30.8 %all-to-all-start.1 = ((bf16[16,48,256]{2,1,0:T(8,128)(2,1)}), bf16[16,48,256]{2,1,0:T(8,128)(2,1)S(1)}, u32[]{:S(2)}, u32[]{:S(2)}) async-start(bf16[16,48,256]{2,1,0:T(8,128)(2,1)} %bitcast.12), calls=%async_computation.1 | async-start | bytes 786432 | tf_op jit(solution)/shard_map/all_to_all | solution.py:1093
  40.7 5.8 %copy-start.1 = (bf16[320,512]{1,0:T(8,128)(2,1)}, bf16[320,512]{1,0:T(8,128)(2,1)S(1)}, u32[]{:S(2)}) copy-start(bf16[320,512]{1,0:T(8,128)(2,1)S(1)} %concatenate.11.own_rel) | copy-start | bytes 983044
  40.7 5.1 %collective-permute-start.6 = (bf16[320,512]{1,0:T(8,128)(2,1)S(1)}, bf16[320,512]{1,0:T(8,128)(2,1)S(1)}, u32[]{:S(2)}, u32[]{:S(2)}) collective-permute-start(bf16[320,512]{1,0:T(8,128)(2,1)S(1)} %concatenate.11.own_rel), channel_id=1, source_target_pairs={{0,16},{16,0},{1,17},{17,1},{2,18},{18,2},{3,19},{19,3},{4,20},{20... | collective-permute-start | bytes 983048 | tf_op jit(solution)/shard_map/ppermute | solution.py:1094
  40.9 21.2 %copy-start = (bf16[80,2432]{1,0:T(8,128)(2,1)}, bf16[80,2432]{1,0:T(8,128)(2,1)S(1)}, u32[]{:S(2)}) copy-start(bf16[80,2432]{1,0:T(8,128)(2,1)S(1)} %pad_maximum_fusion.refs_0_) | copy-start | bytes 1167364
  40.9 21.2 %collective-permute-start.12 = (bf16[80,2432]{1,0:T(8,128)(2,1)S(1)}, bf16[80,2432]{1,0:T(8,128)(2,1)S(1)}, u32[]{:S(2)}, u32[]{:S(2)}) collective-permute-start(bf16[80,2432]{1,0:T(8,128)(2,1)S(1)} %pad_maximum_fusion.refs_0_), channel_id=1, source_target_pairs={{0,3},{1,2},{2,1},{3,0},{4,7},{5,6},{6,5},{7,4},{8,11},{9,10},{10,... | collective-permute-start | bytes 1167368 | tf_op jit(solution)/shard_map/ppermute | solution.py:925
  43.8 20.3 %collective-permute-start.11 = (bf16[80,2432]{1,0:T(8,128)(2,1)S(1)}, bf16[80,2432]{1,0:T(8,128)(2,1)}, u32[]{:S(2)}, u32[]{:S(2)}) collective-permute-start(bf16[80,2432]{1,0:T(8,128)(2,1)S(1)} %pad_maximum_fusion.refs_0_), channel_id=1, source_target_pairs={{0,2},{1,3},{2,0},{3,1},{4,6},{5,7},{6,4},{7,5},{8,10},{9,11},{10,... | collective-permute-start | bytes 1167368 | tf_op jit(solution)/shard_map/ppermute | solution.py:925
  44.4 19.8 %collective-permute-start.10 = (bf16[80,2432]{1,0:T(8,128)(2,1)S(1)}, bf16[80,2432]{1,0:T(8,128)(2,1)}, u32[]{:S(2)}, u32[]{:S(2)}) collective-permute-start(bf16[80,2432]{1,0:T(8,128)(2,1)S(1)} %pad_maximum_fusion.refs_0_), channel_id=1, source_target_pairs={{0,1},{1,0},{2,3},{3,2},{4,5},{5,4},{6,7},{7,6},{8,9},{9,8},{10,11... | collective-permute-start | bytes 1167368 | tf_op jit(solution)/shard_map/ppermute | solution.py:925
  45.8 0.7 copy-start.4
  62.1 7.4 %copy-start.3 = (bf16[80,2432]{1,0:T(8,128)(2,1)}, bf16[80,2432]{1,0:T(8,128)(2,1)S(1)}, u32[]{:S(2)}) copy-start(bf16[80,2432]{1,0:T(8,128)(2,1)S(1)} %collective-permute-done.12.refs_3_) | copy-start | bytes 1167364
  64.1 27.8 %copy-start.2 = (bf16[16,48,256]{2,1,0:T(8,128)(2,1)}, bf16[16,48,256]{2,1,0:T(8,128)(2,1)S(1)}, u32[]{:S(2)}) copy-start(bf16[16,48,256]{2,1,0:T(8,128)(2,1)S(1)} %all-to-all-done.1.refs_1_) | copy-start | bytes 1179652
  64.1 28.5 %all-to-all-start = ((bf16[16,48,640]{2,1,0:T(8,128)(2,1)}), bf16[16,48,640]{2,1,0:T(8,128)(2,1)S(1)}, u32[]{:S(2)}, u32[]{:S(2)}) async-start(bf16[16,48,640]{2,1,0:T(8,128)(2,1)} %bitcast.11), calls=%async_computation | async-start | bytes 1966080 | tf_op jit(solution)/shard_map/all_to_all | solution.py:1163
where the time goes:
time: 99.6 us; the launch traced here: 99 us
  Pallas kernels  62.7 us (63%)
  starting transfers between devices  29.6 us (30%)
  waiting for transfers between devices  2.76 us (3%)
  between operations  2.2 us (2%)
  local copies, waits for them, and re-layouts  1.61 us (2%)
    pallas_call x5, Pallas kernels, call(): pl.pallas_call(kernel, out_shape=[jax.ShapeDtypeStruct(shape, kind) for s...  62.7 us
    ppermute x12, starting transfers between devices, exchange(): parts.append(lax.ppermute(block, axis, route))  17.3 us
    all_to_all x1, starting transfers between devices, body(): lax.all_to_all(turned, 'dp', 0, 0, tiled=True)  7 us
    all_to_all x1, starting transfers between devices, body(): late_all = lax.all_to_all(late, 'dp', 0, 0, tiled=True)  5.3 us
    ppermute x12, waiting for transfers between devices, exchange(): parts.append(lax.ppermute(block, axis, route))  2.06 us
  transfers between devices with their start and end apart: 15, of which 2 were waited for; matrix products, arithmetic and copies ran while one was open for 1% of the time, Pallas kernels for 43%

commit v1 on v0

--- a/solution.py
+++ b/solution.py
@@ -265,9 +265,8 @@
         scores = jnp.where(allowed, s_probs[here, :], -1e30)
         powers = jnp.exp(scores - jnp.max(scores, axis=1, keepdims=True))
         probs = powers * (1.0 / jnp.sum(powers, axis=1, keepdims=True))
-        s_probs[here, :] = probs
         s_low[here, :] = probs.astype(BF16)
-    put_probs = fetch(s_probs, probs_hbm, sems.at[6])
+    put_probs = fetch(s_low, probs_hbm, sems.at[6])
     mixed_wide = mm(s_low[...], s_value[...])
     mixed = mm_tn(repeat, jnp.where(heads, mixed_wide, 0.0).astype(BF16))
     mixed = (mixed * mask).astype(BF16)
@@ -332,9 +331,9 @@
     is_text, width, mask = tower_sizes(full_width, full_hidden)
     get_weight = fetch(triple_hbm.at[0, 1], s_weight, sems.at[0])
     rows = probs_ref.shape[0]
-    low = probs_ref[...].astype(BF16)
+    low = probs_ref[...]
     spread = mm(low, hat_ref[...])
-    spread_ref[...] = spread
+    spread_ref[...] = spread.astype(BF16)
     total = jnp.sum(low.astype(F32), axis=1, keepdims=True)
     s_turn[rows:, :] = jnp.zeros((s_turn.shape[0] - rows, full_width), F32)
     s_turn[0:rows, :] = (spread * ag[...] + total * ab[...]) * mask
@@ -544,8 +543,9 @@
     get_hat.wait()
     get_probs.wait()
     grad_probs = mm_nt((along * gain).astype(BF16), s_hat[...]) + offset
-    probs = s_probs[...]
-    inner = jnp.sum(grad_probs * probs, axis=1, keepdims=True)
+    probs = s_probs[...].astype(F32)
+    prob_total = jnp.sum(probs, axis=1, keepdims=True)
+    inner = jnp.sum(grad_probs * probs, axis=1, keepdims=True) / prob_total
     back = (probs * (grad_probs - inner)).astype(BF16)
     back_ref[...] = back
     spread = mm(back, s_hat[...])
@@ -558,9 +558,8 @@
     rows_one_ref[...] = rows_one
     values_wide = values_low.astype(F32)
     keys_wide = keys_ref[...].astype(F32)
-    prob_total = jnp.sum(probs.astype(BF16).astype(F32), axis=1, keepdims=True)
     gain_sum = (
-        sums_of(values_wide * spread_ref[...])
+        sums_of(values_wide * spread_ref[...].astype(F32))
         + sums_of(keys_wide * spread)
         + sums_of(rows_one * hat_rows_ref[...].astype(F32))
     ) * mask
@@ -642,7 +641,6 @@
         s_vectors,
         s_hat,
         s_inv,
-        s_probs,
         s_left,
         s_right,
         s_early,
@@ -659,7 +657,7 @@
     block = block_rows(all_pairs)
     here = lax.axis_index("dp")
     is_text, width, mask = tower_sizes(full_width, full_hidden)
-    get_probs = fetch(probs_hbm, s_probs, sems.at[3])
+    get_probs = fetch(probs_hbm, s_left.at[pl.ds(0, full_width // HEAD * pairs), :], sems.at[3])
     get_hat = fetch(hat_hbm, s_hat, sems.at[4])
     get_inv = fetch(inv_hbm, s_inv, sems.at[5])
     get_grad = fetch(grad_hbm, grad_ref, sems.at[6])
@@ -682,7 +680,6 @@
     middle_parts = three_parts(rows_mid_ref[...])
     ones = one_hot(iota((full_width, 128), 0).astype(F32) < width)
     get_probs.wait()
-    s_left[0:rows, :] = s_probs[...].astype(BF16)
     get_hat.wait()
     get_inv.wait()
 
@@ -837,20 +834,18 @@
     all_pairs = queries_ref.shape[0]
     s_late[...] = jnp.zeros_like(s_late)
     if not arrived:
-        for source in range(count):
-            now = late_ref[source]
-            s_late[...] += now[:, 0:lanes].astype(F32)
-            means = means_ref[source]
-            across_now = slice(source * pairs, (source + 1) * pairs)
-            for head in range(heads):
-                down = slice(head * slice_width, (head + 1) * slice_width)
-                lane = slice(head * pairs, (head + 1) * pairs)
-                s_keys[down, across_now] = now[:, lane]
-                s_means[down, across_now] = means[:, lane]
-            for slab in range(count):
-                down = slice(slab * slice_width, (slab + 1) * slice_width)
-                first = lanes + slab * pairs
-                s_turned[down, across_now] = now[:, first : first + pairs]
+        sources = range(count)
+        for source in sources:
+            s_late[...] += late_ref[source, :, 0:lanes].astype(F32)
+        for head in range(heads):
+            down = slice(head * slice_width, (head + 1) * slice_width)
+            lane = slice(head * pairs, (head + 1) * pairs)
+            s_keys[down, :] = jnp.concatenate([late_ref[source, :, lane] for source in sources], axis=1)
+            s_means[down, :] = jnp.concatenate([means_ref[source, :, lane] for source in sources], axis=1)
+        for slab in sources:
+            down = slice(slab * slice_width, (slab + 1) * slice_width)
+            lane = slice(lanes + slab * pairs, lanes + (slab + 1) * pairs)
+            s_turned[down, :] = jnp.concatenate([late_ref[source, :, lane] for source in sources], axis=1)
         left = iota((slice_width, 2 * HEAD), 1) < HEAD
         for two in range(heads // 2):
             down = slice(two * 2 * slice_width, (two + 1) * 2 * slice_width)
@@ -1037,7 +1032,7 @@
             ((pairs, 3 * width + 128), BF16),
             ((tokens, width), BF16),
             ((tokens, 128), F32),
-            ((rows, tokens), F32),
+            ((rows, tokens), BF16),
             ((pairs, width), BF16),
             ((pairs, emb), F32),
             ((pairs, width), F32),
@@ -1068,7 +1063,7 @@
         (ends, attention_gain, attention_bias, hat, probs, query, triple_weight),
         [
             ((width, lanes), BF16),
-            ((rows, width), F32),
+            ((rows, width), BF16),
             ((rows, width), BF16),
             ((pairs, width), BF16),
         ],
@@ -1148,7 +1143,7 @@
         + weights_scratch
         + [
             pltpu.VMEM((tokens, width), BF16),
-            pltpu.VMEM((rows, tokens), F32),
+            pltpu.VMEM((rows, tokens), BF16),
             pltpu.VMEM((pairs, emb), F32),
             pltpu.VMEM((pairs, width), F32),
             pltpu.VMEM((lanes, width), F32),
@@ -1236,7 +1231,6 @@
             pltpu.VMEM((8, width), F32),
             pltpu.VMEM((tokens, width), BF16),
             pltpu.VMEM((tokens, 128), F32),
-            pltpu.VMEM((rows, tokens), F32),
             pltpu.VMEM((2 * rows + 3 * pairs, tokens), BF16),
             pltpu.VMEM((2 * rows + 3 * pairs, width), BF16),
             pltpu.VMEM((all_pairs, 3 * width + 128), BF16),

time: 99.6 us -> 97.5 us (0.979)
  Pallas kernels: 62.7 us -> 59.5 us
  waiting for transfers between devices: 2.76 us -> 3.98 us
    pallas_call x5, Pallas kernels: 62.7 us -> 59.5 us  [call(): pl.pallas_call(kernel, out_shape=[jax.ShapeDtypeStruct(shape, kind) for s...]
    all_to_all x1, waiting for transfers between devices: 0.69 us -> 1.81 us  [body(): late_all = lax.all_to_all(late, 'dp', 0, 0, tiled=True)]
  transfers between devices with their start and end apart: 15 -> 15, of which waited for: 2 -> 2; matrix products, arithmetic and copies ran while one was open for 1% -> 1% of each run, Pallas kernels for 43% -> 42%
where the time goes in v1:
time: 97.5 us; the launch traced here: 97 us
  Pallas kernels  59.5 us (61%)
  starting transfers between devices  29.6 us (30%)
  waiting for transfers between devices  3.98 us (4%)
  between operations  2.19 us (2%)
  local copies, waits for them, and re-layouts  1.62 us (2%)
    pallas_call x5, Pallas kernels, call(): pl.pallas_call(kernel, out_shape=[jax.ShapeDtypeStruct(shape, kind) for s...  59.5 us
    ppermute x12, starting transfers between devices, exchange(): parts.append(lax.ppermute(block, axis, route))  17.3 us
    all_to_all x1, starting transfers between devices, body(): lax.all_to_all(turned, 'dp', 0, 0, tiled=True)  7.02 us
    all_to_all x1, starting transfers between devices, body(): late_all = lax.all_to_all(late, 'dp', 0, 0, tiled=True)  5.27 us
    ppermute x12, waiting for transfers between devices, exchange(): parts.append(lax.ppermute(block, axis, route))  2.16 us
  transfers between devices with their start and end apart: 15, of which 2 were waited for; matrix products, arithmetic and copies ran while one was open for 1% of the time, Pallas kernels for 42%

profile of v1, /device:TPU:0, one launch (start us, length us, event | category | flops | bytes accessed | tf_op | source)
XLA Modules:
  0.0 97.0 jit_solution(9874308367775327054)
XLA Ops:
  0.7 13.8 %shard_map.339 = (bf16[20,512]{1,0:T(8,128)(2,1)}, bf16[20,2432]{1,0:T(8,128)(2,1)}, bf16[1080,768]{1,0:T(8,128)(2,1)}, f32[1080,128]{1,0:T(8,128)}, bf16[240,10...) custom-call(s32[1,20]{1,0:T(1,128)} %bitcast.13, ...), custom_call_target="tpu_custom_call" | custom-call | flops 1000000000 | bytes 20000000 | tf_op jit(solution)/shard_map/pallas_call | solution.py:939
  14.5 0.0 copy-start.7
  14.5 0.0 copy-start.6
  14.5 0.0 copy-start.5
  14.5 5.1 %collective-permute-start.2 = (bf16[20,512]{1,0:T(8,128)(2,1)}, bf16[20,512]{1,0:T(8,128)(2,1)S(1)}, u32[]{:S(2)}, u32[]{:S(2)}) collective-permute-start(bf16[20,512]{1,0:T(8,128)(2,1)} %get-tuple-element.86), channel_id=1, source_target_pairs={{0,12},{1,13},{2,14},{3,15},{4,8},{5,9},{6,10},{7,11},{8,4},{9,5},... | collective-permute-start | bytes 61448 | tf_op jit(solution)/shard_map/ppermute | solution.py:920
  19.6 0.0 collective-permute-start.1
  19.6 0.6 collective-permute-start
  20.3 4.2 %shard_map.340 = (bf16[768,256]{1,0:T(8,128)(2,1)}, bf16[240,768]{1,0:T(8,128)(2,1)}, bf16[240,768]{1,0:T(8,128)(2,1)}, bf16[20,768]{1,0:T(8,128)(2,1)}) custom-call(s32[1,20]{1,0:T(1,128)} %bitcast.14, f32[1,768]{1,0:T(1,128)} %refs_14_.1, f32[1,768]{1,0:T(1,128)} %refs_15_.1, bf16[1080,768]{1,0:T(8,128)(2,1)} %get-tuple-element.79.hat_ref.hat_hbm.refs_5_, ...), custom_call_target="tpu_custom_call" | custom-call | flops 1000000000 | bytes 5000000 | tf_op jit(solution)/shard_map/pallas_call | solution.py:939
  24.5 0.0 copy-done.7
  24.5 0.5 reshape.59.flags_ref
  25.1 0.0 collective-permute-done.2
  25.1 0.0 collective-permute-done.1
  25.1 0.0 collective-permute-done
  25.1 0.0 copy-done.6
  25.1 2.7 %collective-permute-start.5 = (bf16[80,512]{1,0:T(8,128)(2,1)S(1)}, bf16[80,512]{1,0:T(8,128)(2,1)S(1)}, u32[]{:S(2)}, u32[]{:S(2)}) collective-permute-start(bf16[80,512]{1,0:T(8,128)(2,1)S(1)} %pad_maximum_fusion.1), channel_id=1, source_target_pairs={{0,3},{1,2},{2,1},{3,0},{4,7},{5,6},{6,5},{7,4},{8,11},{9,10},{10,... | collective-permute-start | bytes 245768 | tf_op jit(solution)/shard_map/ppermute | solution.py:920
  27.8 0.0 copy-done.5
  27.8 3.6 %collective-permute-start.9 = (bf16[20,2432]{1,0:T(8,128)(2,1)S(1)}, bf16[20,2432]{1,0:T(8,128)(2,1)S(1)}, u32[]{:S(2)}, u32[]{:S(2)}) collective-permute-start(bf16[20,2432]{1,0:T(8,128)(2,1)S(1)} %copy-done.5), channel_id=1, source_target_pairs={{0,12},{1,13},{2,14},{3,15},{4,8},{5,9},{6,10},{7,11},{8,4},{9,5},... | collective-permute-start | bytes 291848 | tf_op jit(solution)/shard_map/ppermute | solution.py:920
  31.4 0.0 collective-permute-start.8
  31.4 0.8 collective-permute-start.7
  32.2 0.5 collective-permute-start.4
  32.7 0.0 collective-permute-done.5
  32.7 0.4 collective-permute-start.3
  33.1 7.0 %all-to-all-start.1 = ((bf16[16,48,256]{2,1,0:T(8,128)(2,1)}), bf16[16,48,256]{2,1,0:T(8,128)(2,1)S(1)}, u32[]{:S(2)}, u32[]{:S(2)}) async-start(bf16[16,48,256]{2,1,0:T(8,128)(2,1)} %bitcast.12), calls=%async_computation.1 | async-start | bytes 786432 | tf_op jit(solution)/shard_map/all_to_all | solution.py:1088
  40.1 0.0 collective-permute-done.4
  40.1 0.0 collective-permute-done.3
  40.1 0.3 concatenate.11.own_rel
  40.5 0.0 copy-start.1
  40.5 0.1 collective-permute-start.6
  40.6 0.0 collective-permute-done.9
  40.6 0.0 collective-permute-done.8
  40.6 0.0 collective-permute-done.7
  40.6 0.1 pad_maximum_fusion.refs_0_
  40.7 0.0 copy-start
  40.7 2.9 %collective-permute-start.12 = (bf16[80,2432]{1,0:T(8,128)(2,1)S(1)}, bf16[80,2432]{1,0:T(8,128)(2,1)S(1)}, u32[]{:S(2)}, u32[]{:S(2)}) collective-permute-start(bf16[80,2432]{1,0:T(8,128)(2,1)S(1)} %pad_maximum_fusion.refs_0_), channel_id=1, source_target_pairs={{0,3},{1,2},{2,1},{3,0},{4,7},{5,6},{6,5},{7,4},{8,11},{9,10},{10,... | collective-permute-start | bytes 1167368 | tf_op jit(solution)/shard_map/ppermute | solution.py:920
  43.6 0.6 collective-permute-start.11
  44.1 0.1 collective-permute-start.10
  45.5 0.0 collective-permute-done.6.other_rel
  45.6 0.0 copy-start.4
  45.6 0.7 copy-done.4
  46.3 15.5 %shard_map.341 = (f32[1,1]{1,0:T(1,128)}, f32[1,1]{1,0:T(1,128)}, f32[1,1]{1,0:T(1,128)}, f32[320,512]{1,0:T(8,128)}, bf16[768,640]{1,0:T(8,128)(2,1)}, /*index=...) custom-call(bf16[320,512]{1,0:T(8,128)(2,1)} %copy-done.1, ...), custom_call_target="tpu_custom_call" | custom-call | flops 1000000000 | bytes 20000000 | tf_op jit(solution)/shard_map/pallas_call | solution.py:939
  61.8 0.0 collective-permute-done.12.refs_3_
  61.8 2.1 %collective-permute-done.11.refs_2_ = bf16[80,2432]{1,0:T(8,128)(2,1)} collective-permute-done((bf16[80,2432]{1,0:T(8,128)(2,1)S(1)}, bf16[80,2432]{1,0:T(8,128)(2,1)}, u32[]{:S(2)}, u32[]{:S(2)}) %collective-permute-start.11) | collective-permute-done | bytes 389152 | tf_op jit(solution)/shard_map/ppermute | solution.py:920
  63.9 0.0 collective-permute-done.10.refs_1_
  63.9 0.0 all-to-all-done.1.refs_1_
  63.9 5.3 %all-to-all-start = ((bf16[16,48,640]{2,1,0:T(8,128)(2,1)}), bf16[16,48,640]{2,1,0:T(8,128)(2,1)S(1)}, u32[]{:S(2)}, u32[]{:S(2)}) async-start(bf16[16,48,640]{2,1,0:T(8,128)(2,1)} %bitcast.11), calls=%async_computation | async-start | bytes 1966080 | tf_op jit(solution)/shard_map/all_to_all | solution.py:1158
  69.2 21.4 %shard_map.342 = (f32[1,1080,768]{2,1,0:T(8,128)}, bf16[320,48]{1,0:T(8,128)(2,1)}, bf16[320,768]{1,0:T(8,128)(2,1)}, bf16[320,768]{1,0:T(8,128)(2,1)}, f32[1,48...) custom-call(bf16[80,2432]{1,0:T(8,128)(2,1)} %copy-done, ...), custom_call_target="tpu_custom_call" | custom-call | flops 3000000000 | bytes 10000000 | tf_op jit(solution)/shard_map/pallas_call | solution.py:939
  90.6 1.8 %all-to-all-done.refs_0_ = bf16[16,48,640]{2,1,0:T(8,128)(2,1)S(1)} async-done(((bf16[16,48,640]{2,1,0:T(8,128)(2,1)}), bf16[16,48,640]{2,1,0:T(8,128)(2,1)S(1)}, u32[]{:S(2)}, u32[]{:S(2)}) %all-to-all-start) | async-done | bytes 983072 | tf_op jit(solution)/shard_map/all_to_all | solution.py:1158
  92.5 4.6 %shard_map.343 = (f32[1,3,48,768]{3,2,1,0:T(8,128)}, f32[1,48]{1,0:T(1,128)}, f32[1,48]{1,0:T(1,128)}, f32[1,2,48]{2,1,0:T(2,128)}) custom-call(bf16[16,48,640]{2,1,0:T(8,128)(2,1)S(1)} %all-to-all-done.refs_0_, bf16[16,48,256]{2,1,0:T(8,128)(2,1)} %copy-done.2, bf16[320,48]{1,0:T(8,128)(2,1)} %get-tuple-element.115.refs_2_, ...), custom_call_target="tpu_custom_call" | custom-call | flops 1000000000 | bytes 10000000 | tf_op jit(solution)/shard_map/pallas_call | solution.py:939
  (7 shorter events, 0.0 us)
Async XLA Ops:
  14.5 10.0 %copy-start.7 = (s32[320]{0:T(512)S(1)}, s32[320]{0:T(512)}, u32[]{:S(2)}) copy-start(s32[320]{0:T(512)} %param.23) | copy-start | bytes 3844
  14.5 10.6 %copy-start.6 = (bf16[20,512]{1,0:T(8,128)(2,1)S(1)}, bf16[20,512]{1,0:T(8,128)(2,1)}, u32[]{:S(2)}) copy-start(bf16[20,512]{1,0:T(8,128)(2,1)} %get-tuple-element.86) | copy-start | bytes 61444
  14.5 13.3 %copy-start.5 = (bf16[20,2432]{1,0:T(8,128)(2,1)S(1)}, bf16[20,2432]{1,0:T(8,128)(2,1)}, u32[]{:S(2)}) copy-start(bf16[20,2432]{1,0:T(8,128)(2,1)} %get-tuple-element.100) | copy-start | bytes 291844
  14.5 10.5 %collective-permute-start.2 = (bf16[20,512]{1,0:T(8,128)(2,1)}, bf16[20,512]{1,0:T(8,128)(2,1)S(1)}, u32[]{:S(2)}, u32[]{:S(2)}) collective-permute-start(bf16[20,512]{1,0:T(8,128)(2,1)} %get-tuple-element.86), channel_id=1, source_target_pairs={{0,12},{1,13},{2,14},{3,15},{4,8},{5,9},{6,10},{7,11},{8,4},{9,5},... | collective-permute-start | bytes 61448 | tf_op jit(solution)/shard_map/ppermute | solution.py:920
  19.6 5.4 %collective-permute-start.1 = (bf16[20,512]{1,0:T(8,128)(2,1)}, bf16[20,512]{1,0:T(8,128)(2,1)S(1)}, u32[]{:S(2)}, u32[]{:S(2)}) collective-permute-start(bf16[20,512]{1,0:T(8,128)(2,1)} %get-tuple-element.86), channel_id=1, source_target_pairs={{0,8},{1,9},{2,10},{3,11},{4,12},{5,13},{6,14},{7,15},{8,0},{9,1},... | collective-permute-start | bytes 61448 | tf_op jit(solution)/shard_map/ppermute | solution.py:920
  19.6 5.4 %collective-permute-start = (bf16[20,512]{1,0:T(8,128)(2,1)}, bf16[20,512]{1,0:T(8,128)(2,1)S(1)}, u32[]{:S(2)}, u32[]{:S(2)}) collective-permute-start(bf16[20,512]{1,0:T(8,128)(2,1)} %get-tuple-element.86), channel_id=1, source_target_pairs={{0,4},{1,5},{2,6},{3,7},{4,0},{5,1},{6,2},{7,3},{8,12},{9,13},{10,... | collective-permute-start | bytes 61448 | tf_op jit(solution)/shard_map/ppermute | solution.py:920
  25.1 7.6 %collective-permute-start.5 = (bf16[80,512]{1,0:T(8,128)(2,1)S(1)}, bf16[80,512]{1,0:T(8,128)(2,1)S(1)}, u32[]{:S(2)}, u32[]{:S(2)}) collective-permute-start(bf16[80,512]{1,0:T(8,128)(2,1)S(1)} %pad_maximum_fusion.1), channel_id=1, source_target_pairs={{0,3},{1,2},{2,1},{3,0},{4,7},{5,6},{6,5},{7,4},{8,11},{9,10},{10,... | collective-permute-start | bytes 245768 | tf_op jit(solution)/shard_map/ppermute | solution.py:920
  27.8 12.8 %collective-permute-start.9 = (bf16[20,2432]{1,0:T(8,128)(2,1)S(1)}, bf16[20,2432]{1,0:T(8,128)(2,1)S(1)}, u32[]{:S(2)}, u32[]{:S(2)}) collective-permute-start(bf16[20,2432]{1,0:T(8,128)(2,1)S(1)} %copy-done.5), channel_id=1, source_target_pairs={{0,12},{1,13},{2,14},{3,15},{4,8},{5,9},{6,10},{7,11},{8,4},{9,5},... | collective-permute-start | bytes 291848 | tf_op jit(solution)/shard_map/ppermute | solution.py:920
  31.4 9.2 %collective-permute-start.8 = (bf16[20,2432]{1,0:T(8,128)(2,1)S(1)}, bf16[20,2432]{1,0:T(8,128)(2,1)S(1)}, u32[]{:S(2)}, u32[]{:S(2)}) collective-permute-start(bf16[20,2432]{1,0:T(8,128)(2,1)S(1)} %copy-done.5), channel_id=1, source_target_pairs={{0,8},{1,9},{2,10},{3,11},{4,12},{5,13},{6,14},{7,15},{8,0},{9,1},... | collective-permute-start | bytes 291848 | tf_op jit(solution)/shard_map/ppermute | solution.py:920
  31.4 9.2 %collective-permute-start.7 = (bf16[20,2432]{1,0:T(8,128)(2,1)S(1)}, bf16[20,2432]{1,0:T(8,128)(2,1)S(1)}, u32[]{:S(2)}, u32[]{:S(2)}) collective-permute-start(bf16[20,2432]{1,0:T(8,128)(2,1)S(1)} %copy-done.5), channel_id=1, source_target_pairs={{0,4},{1,5},{2,6},{3,7},{4,0},{5,1},{6,2},{7,3},{8,12},{9,13},{10,... | collective-permute-start | bytes 291848 | tf_op jit(solution)/shard_map/ppermute | solution.py:920
  32.2 7.9 %collective-permute-start.4 = (bf16[80,512]{1,0:T(8,128)(2,1)S(1)}, bf16[80,512]{1,0:T(8,128)(2,1)S(1)}, u32[]{:S(2)}, u32[]{:S(2)}) collective-permute-start(bf16[80,512]{1,0:T(8,128)(2,1)S(1)} %pad_maximum_fusion.1), channel_id=1, source_target_pairs={{0,2},{1,3},{2,0},{3,1},{4,6},{5,7},{6,4},{7,5},{8,10},{9,11},{10,... | collective-permute-start | bytes 245768 | tf_op jit(solution)/shard_map/ppermute | solution.py:920
  32.7 7.4 %collective-permute-start.3 = (bf16[80,512]{1,0:T(8,128)(2,1)S(1)}, bf16[80,512]{1,0:T(8,128)(2,1)S(1)}, u32[]{:S(2)}, u32[]{:S(2)}) collective-permute-start(bf16[80,512]{1,0:T(8,128)(2,1)S(1)} %pad_maximum_fusion.1), channel_id=1, source_target_pairs={{0,1},{1,0},{2,3},{3,2},{4,5},{5,4},{6,7},{7,6},{8,9},{9,8},{10,11... | collective-permute-start | bytes 245768 | tf_op jit(solution)/shard_map/ppermute | solution.py:920
  33.1 30.9 %all-to-all-start.1 = ((bf16[16,48,256]{2,1,0:T(8,128)(2,1)}), bf16[16,48,256]{2,1,0:T(8,128)(2,1)S(1)}, u32[]{:S(2)}, u32[]{:S(2)}) async-start(bf16[16,48,256]{2,1,0:T(8,128)(2,1)} %bitcast.12), calls=%async_computation.1 | async-start | bytes 786432 | tf_op jit(solution)/shard_map/all_to_all | solution.py:1088
  40.5 5.8 %copy-start.1 = (bf16[320,512]{1,0:T(8,128)(2,1)}, bf16[320,512]{1,0:T(8,128)(2,1)S(1)}, u32[]{:S(2)}) copy-start(bf16[320,512]{1,0:T(8,128)(2,1)S(1)} %concatenate.11.own_rel) | copy-start | bytes 983044
  40.5 5.1 %collective-permute-start.6 = (bf16[320,512]{1,0:T(8,128)(2,1)S(1)}, bf16[320,512]{1,0:T(8,128)(2,1)S(1)}, u32[]{:S(2)}, u32[]{:S(2)}) collective-permute-start(bf16[320,512]{1,0:T(8,128)(2,1)S(1)} %concatenate.11.own_rel), channel_id=1, source_target_pairs={{0,16},{16,0},{1,17},{17,1},{2,18},{18,2},{3,19},{19,3},{4,20},{20... | collective-permute-start | bytes 983048 | tf_op jit(solution)/shard_map/ppermute | solution.py:1089
  40.7 21.1 %copy-start = (bf16[80,2432]{1,0:T(8,128)(2,1)}, bf16[80,2432]{1,0:T(8,128)(2,1)S(1)}, u32[]{:S(2)}) copy-start(bf16[80,2432]{1,0:T(8,128)(2,1)S(1)} %pad_maximum_fusion.refs_0_) | copy-start | bytes 1167364
  40.7 21.1 %collective-permute-start.12 = (bf16[80,2432]{1,0:T(8,128)(2,1)S(1)}, bf16[80,2432]{1,0:T(8,128)(2,1)S(1)}, u32[]{:S(2)}, u32[]{:S(2)}) collective-permute-start(bf16[80,2432]{1,0:T(8,128)(2,1)S(1)} %pad_maximum_fusion.refs_0_), channel_id=1, source_target_pairs={{0,3},{1,2},{2,1},{3,0},{4,7},{5,6},{6,5},{7,4},{8,11},{9,10},{10,... | collective-permute-start | bytes 1167368 | tf_op jit(solution)/shard_map/ppermute | solution.py:920
  43.6 20.3 %collective-permute-start.11 = (bf16[80,2432]{1,0:T(8,128)(2,1)S(1)}, bf16[80,2432]{1,0:T(8,128)(2,1)}, u32[]{:S(2)}, u32[]{:S(2)}) collective-permute-start(bf16[80,2432]{1,0:T(8,128)(2,1)S(1)} %pad_maximum_fusion.refs_0_), channel_id=1, source_target_pairs={{0,2},{1,3},{2,0},{3,1},{4,6},{5,7},{6,4},{7,5},{8,10},{9,11},{10,... | collective-permute-start | bytes 1167368 | tf_op jit(solution)/shard_map/ppermute | solution.py:920
  44.1 19.8 %collective-permute-start.10 = (bf16[80,2432]{1,0:T(8,128)(2,1)S(1)}, bf16[80,2432]{1,0:T(8,128)(2,1)}, u32[]{:S(2)}, u32[]{:S(2)}) collective-permute-start(bf16[80,2432]{1,0:T(8,128)(2,1)S(1)} %pad_maximum_fusion.refs_0_), channel_id=1, source_target_pairs={{0,1},{1,0},{2,3},{3,2},{4,5},{5,4},{6,7},{7,6},{8,9},{9,8},{10,11... | collective-permute-start | bytes 1167368 | tf_op jit(solution)/shard_map/ppermute | solution.py:920
  45.6 0.7 copy-start.4
  61.8 7.4 %copy-start.3 = (bf16[80,2432]{1,0:T(8,128)(2,1)}, bf16[80,2432]{1,0:T(8,128)(2,1)S(1)}, u32[]{:S(2)}) copy-start(bf16[80,2432]{1,0:T(8,128)(2,1)S(1)} %collective-permute-done.12.refs_3_) | copy-start | bytes 1167364
  63.9 26.7 %copy-start.2 = (bf16[16,48,256]{2,1,0:T(8,128)(2,1)}, bf16[16,48,256]{2,1,0:T(8,128)(2,1)S(1)}, u32[]{:S(2)}) copy-start(bf16[16,48,256]{2,1,0:T(8,128)(2,1)S(1)} %all-to-all-done.1.refs_1_) | copy-start | bytes 1179652
  63.9 28.5 %all-to-all-start = ((bf16[16,48,640]{2,1,0:T(8,128)(2,1)}), bf16[16,48,640]{2,1,0:T(8,128)(2,1)S(1)}, u32[]{:S(2)}, u32[]{:S(2)}) async-start(bf16[16,48,640]{2,1,0:T(8,128)(2,1)} %bitcast.11), calls=%async_computation | async-start | bytes 1966080 | tf_op jit(solution)/shard_map/all_to_all | solution.py:1158

commit v2 on v1

--- a/solution.py
+++ b/solution.py
@@ -602,6 +602,7 @@
         keys_ref,
         rows_one_ref,
         rows_mid_ref,
+        means_ref,
         grad_hbm,
         ag,
         ab,
@@ -633,6 +634,7 @@
         mixer_bias_ref,
         value_bias_ref,
         widen_bias_ref,
+        value_weight_ref,
         s_triple,
         s_wo,
         s_ww,
@@ -649,6 +651,7 @@
         s_total,
         s_active,
         s_hidden,
+        s_means,
         sems,
         hidden_sems,
         out_sems,
@@ -791,6 +794,16 @@
             hidden.wait(chunk)
     over_blocks(all_pairs // block, part)
     over_tokens(tokens, NORM_ROWS, lambda at, count: put(at, count).wait())
+    count = means_ref.shape[0]
+    if count <= 16 and slice_width % 16 == 0:
+        from_heads(
+            [means_ref.at[source] for source in range(count)],
+            values_ref,
+            value_weight_ref,
+            s_means,
+            pairs,
+            slice_width,
+        )
     vectors = dot_dims(s_vectors[...], pick.astype(F32), 1, 0, lax.Precision.HIGHEST)
     for slot, ref in enumerate(
         (
@@ -806,6 +819,20 @@
         ref[...] = vectors[slot : slot + 1, :]
 
 
+def from_heads(sources, right_ref, out_ref, s_left, pairs, slice_width):
+    heads = right_ref.shape[1] // HEAD
+    for head in range(heads):
+        down = slice(head * slice_width, (head + 1) * slice_width)
+        lane = slice(head * pairs, (head + 1) * pairs)
+        s_left[down, :] = jnp.concatenate([source[:, lane] for source in sources], axis=1)
+    left = iota((slice_width, 2 * HEAD), 1) < HEAD
+    for two in range(heads // 2):
+        down = slice(two * 2 * slice_width, (two + 1) * 2 * slice_width)
+        lane = slice(two * 2 * HEAD, (two + 1) * 2 * HEAD)
+        both = mm(s_left[down, :], right_ref[:, lane])
+        out_ref[:, lane] = jnp.where(left, both[0:slice_width], both[slice_width:])
+
+
 def last_kernel(dims, *refs):
     pairs, full_width, full_hidden, slice_width, stages, pieces = dims
     arrived = refs[:pieces]
@@ -816,19 +843,19 @@
         queries_ref,
         values_ref,
         value_bias_ref,
+        value_weight_ref,
         triple_ref,
         gain_ref,
         shift_ref,
         bias_ref,
         s_keys,
-        s_means,
         s_turned,
         s_late,
         s_sums,
     ) = refs[pieces:]
     here = lax.axis_index("dp")
     count = late_ref.shape[0]
-    lanes = means_ref.shape[2]
+    lanes = -(-(full_width // HEAD * pairs + 12) // 128) * 128
     heads = full_width // HEAD
     rows = heads * pairs
     all_pairs = queries_ref.shape[0]
@@ -837,23 +864,20 @@
         sources = range(count)
         for source in sources:
             s_late[...] += late_ref[source, :, 0:lanes].astype(F32)
-        for head in range(heads):
-            down = slice(head * slice_width, (head + 1) * slice_width)
-            lane = slice(head * pairs, (head + 1) * pairs)
-            s_keys[down, :] = jnp.concatenate([late_ref[source, :, lane] for source in sources], axis=1)
-            s_means[down, :] = jnp.concatenate([means_ref[source, :, lane] for source in sources], axis=1)
+        from_heads(
+            [late_ref.at[source] for source in sources],
+            queries_ref,
+            triple_ref.at[0, 1],
+            s_keys,
+            pairs,
+            slice_width,
+        )
+        triple_ref[0, 1] = triple_ref[0, 1] * 0.125
+        triple_ref[0, 2] = value_weight_ref[...]
         for slab in sources:
             down = slice(slab * slice_width, (slab + 1) * slice_width)
             lane = slice(lanes + slab * pairs, lanes + (slab + 1) * pairs)
             s_turned[down, :] = jnp.concatenate([late_ref[source, :, lane] for source in sources], axis=1)
-        left = iota((slice_width, 2 * HEAD), 1) < HEAD
-        for two in range(heads // 2):
-            down = slice(two * 2 * slice_width, (two + 1) * 2 * slice_width)
-            lane = slice(two * 2 * HEAD, (two + 1) * 2 * HEAD)
-            both = mm(s_keys[down, :], queries_ref[:, lane]) * 0.125
-            triple_ref[0, 1, :, lane] = jnp.where(left, both[0:slice_width], both[slice_width:])
-            both = mm(s_means[down, :], values_ref[:, lane])
-            triple_ref[0, 2, :, lane] = jnp.where(left, both[0:slice_width], both[slice_width:])
         triple_ref[0, 0] = mm(s_turned[...], ones_ref[...]).T
         mine = s_turned[pl.ds(pl.multiple_of(here * slice_width, slice_width), slice_width), :]
         sums = mm_nt(jnp.ones((8, all_pairs), BF16), mine)
@@ -1080,8 +1104,8 @@
     for index, stage in enumerate(stages):
         own_parts = exchange(own_rel, "dp", stage)
         if index + 1 < len(stages):
-            own_parts, early_rows, turned, spread, keys, hat_rows, flags = lax.optimization_barrier(
-                (own_parts, early_rows, turned, spread, keys, hat_rows, flags)
+            own_parts, early_rows, turned, spread, keys, hat_rows = lax.optimization_barrier(
+                (own_parts, early_rows, turned, spread, keys, hat_rows)
             )
             early_rows = jnp.concatenate(exchange(early_rows, "dp", stage), axis=0)
         own_rel = jnp.concatenate(own_parts, axis=0)
@@ -1181,6 +1205,7 @@
         grad_mixer_bias,
         grad_value_bias,
         grad_widen_bias,
+        grad_value_weight,
     ) = call(
         partial(
             rows_kernel,
@@ -1197,6 +1222,7 @@
             keys,
             rows_one,
             rows_mid,
+            means_all,
             grad_all,
             attention_gain,
             attention_bias,
@@ -1224,7 +1250,7 @@
             ((1, slice_width, width), F32),
         ]
         + [vector] * 7
-        + [((1, slice_hidden), F32)],
+        + [((1, slice_hidden), F32), ((slice_width, width), F32)],
         [pltpu.VMEM((width, width), BF16)]
         + weights_scratch[1:]
         + [
@@ -1239,18 +1265,19 @@
             pltpu.VMEM((block_rows(all_pairs), width), F32),
             pltpu.VMEM((block_rows(all_pairs), slice_hidden), F32),
             pltpu.VMEM((block_rows(all_pairs), slice_hidden), F32),
+            pltpu.VMEM((width // HEAD * slice_width if compact else 16, all_pairs), BF16),
             dma((7 + ahead,)),
             dma((2, chunk_count)),
             dma((-(-tokens // NORM_ROWS),)),
         ],
-        in_hbm=tuple(range(ahead)) + tuple(ahead + index for index in (1, 2, 3, 9, 12, 14, 18, 20, 23)),
+        in_hbm=tuple(range(ahead)) + tuple(ahead + index for index in (1, 2, 3, 10, 13, 15, 19, 21, 24)),
         out_hbm=(0,),
         cost=(3 * 10**9, 10 * 10**6),
     )
     grad_triple, grad_gain, grad_bias, grad_triple_bias = call(
         partial(last_kernel, (pairs, width, hidden, slice_width, stages, len(late_pieces))),
         tuple(late_pieces)
-        + (late_all, means_all, ones, query_rows, value_rows, grad_value_bias),
+        + (late_all, means_all, ones, query_rows, value_rows, grad_value_bias, grad_value_weight),
         [
             ((1, 3, slice_width, width), F32),
             vector,
@@ -1259,12 +1286,12 @@
         ],
         [
             pltpu.VMEM((width // HEAD * slice_width, all_pairs), BF16),
-            pltpu.VMEM((width // HEAD * slice_width, all_pairs), BF16),
             pltpu.VMEM((width, all_pairs), BF16),
             pltpu.VMEM((slice_width, lanes), F32),
             pltpu.VMEM((8, width), F32),
         ],
         cost=(10**9, 10 * 10**6),
+        in_hbm=(1, 4) if compact else (),
         kept=(0,) if compact else (),
         limit=32 * 1024 * 1024 if compact else VMEM_LIMIT,
     )

time: 97.5 us -> 96.2 us (0.987)
  waiting for transfers between devices: 3.98 us -> 1.66 us
    all_to_all x1, waiting for transfers between devices: 1.81 us -> 0.01 us  [body(): late_all = lax.all_to_all(late, 'dp', 0, 0, tiled=True)]
  transfers between devices with their start and end apart: 15 -> 15, of which waited for: 2 -> 1; matrix products, arithmetic and copies ran while one was open for 1% -> 1% of each run, Pallas kernels for 42% -> 45%
where the time goes in v2:
time: 96.2 us; the launch traced here: 95.7 us
  Pallas kernels  60.4 us (63%)
  starting transfers between devices  29.7 us (31%)
  between operations  2.17 us (2%)
  waiting for transfers between devices  1.66 us (2%)
  local copies, waits for them, and re-layouts  1.61 us (2%)
    pallas_call x5, Pallas kernels, call(): pl.pallas_call(kernel, out_shape=[jax.ShapeDtypeStruct(shape, kind) for s...  60.4 us
    ppermute x12, starting transfers between devices, exchange(): parts.append(lax.ppermute(block, axis, route))  17.3 us
    all_to_all x1, starting transfers between devices, body(): lax.all_to_all(turned, 'dp', 0, 0, tiled=True)  7.01 us
    all_to_all x1, starting transfers between devices, body(): late_all = lax.all_to_all(late, 'dp', 0, 0, tiled=True)  5.35 us
  transfers between devices with their start and end apart: 15, of which 1 were waited for; matrix products, arithmetic and copies ran while one was open for 1% of the time, Pallas kernels for 45%

profile of v2, /device:TPU:0, one launch (start us, length us, event | category | flops | bytes accessed | tf_op | source)
XLA Modules:
  0.0 95.7 jit_solution(11470820928099950083)
XLA Ops:
  0.7 13.8 %shard_map.339 = (bf16[20,512]{1,0:T(8,128)(2,1)}, bf16[20,2432]{1,0:T(8,128)(2,1)}, bf16[1080,768]{1,0:T(8,128)(2,1)}, f32[1080,128]{1,0:T(8,128)}, bf16[240,10...) custom-call(s32[1,20]{1,0:T(1,128)} %bitcast.13, ...), custom_call_target="tpu_custom_call" | custom-call | flops 1000000000 | bytes 20000000 | tf_op jit(solution)/shard_map/pallas_call | solution.py:963
  14.5 0.0 copy-start.6
  14.5 0.0 copy-start.5
  14.5 5.1 %collective-permute-start.2 = (bf16[20,512]{1,0:T(8,128)(2,1)}, bf16[20,512]{1,0:T(8,128)(2,1)S(1)}, u32[]{:S(2)}, u32[]{:S(2)}) collective-permute-start(bf16[20,512]{1,0:T(8,128)(2,1)} %get-tuple-element.86), channel_id=1, source_target_pairs={{0,12},{1,13},{2,14},{3,15},{4,8},{5,9},{6,10},{7,11},{8,4},{9,5},... | collective-permute-start | bytes 61448 | tf_op jit(solution)/shard_map/ppermute | solution.py:944
  19.6 0.0 collective-permute-start.1
  19.6 0.6 collective-permute-start
  20.3 4.2 %shard_map.340 = (bf16[768,256]{1,0:T(8,128)(2,1)}, bf16[240,768]{1,0:T(8,128)(2,1)}, bf16[240,768]{1,0:T(8,128)(2,1)}, bf16[20,768]{1,0:T(8,128)(2,1)}) custom-call(s32[1,20]{1,0:T(1,128)} %bitcast.14, f32[1,768]{1,0:T(1,128)} %refs_15_.1, f32[1,768]{1,0:T(1,128)} %refs_16_.1, bf16[1080,768]{1,0:T(8,128)(2,1)} %get-tuple-element.79.hat_ref.hat_hbm.refs_5_, ...), custom_call_target="tpu_custom_call" | custom-call | flops 1000000000 | bytes 5000000 | tf_op jit(solution)/shard_map/pallas_call | solution.py:963
  24.5 0.0 collective-permute-done.2
  24.5 0.0 collective-permute-done.1
  24.6 0.0 collective-permute-done
  24.6 0.0 copy-done.6
  24.6 2.7 %collective-permute-start.5 = (bf16[80,512]{1,0:T(8,128)(2,1)S(1)}, bf16[80,512]{1,0:T(8,128)(2,1)S(1)}, u32[]{:S(2)}, u32[]{:S(2)}) collective-permute-start(bf16[80,512]{1,0:T(8,128)(2,1)S(1)} %pad_maximum_fusion.1), channel_id=1, source_target_pairs={{0,3},{1,2},{2,1},{3,0},{4,7},{5,6},{6,5},{7,4},{8,11},{9,10},{10,... | collective-permute-start | bytes 245768 | tf_op jit(solution)/shard_map/ppermute | solution.py:944
  27.2 0.0 copy-done.5
  27.3 3.6 %collective-permute-start.9 = (bf16[20,2432]{1,0:T(8,128)(2,1)S(1)}, bf16[20,2432]{1,0:T(8,128)(2,1)S(1)}, u32[]{:S(2)}, u32[]{:S(2)}) collective-permute-start(bf16[20,2432]{1,0:T(8,128)(2,1)S(1)} %copy-done.5), channel_id=1, source_target_pairs={{0,12},{1,13},{2,14},{3,15},{4,8},{5,9},{6,10},{7,11},{8,4},{9,5},... | collective-permute-start | bytes 291848 | tf_op jit(solution)/shard_map/ppermute | solution.py:944
  30.9 0.0 collective-permute-start.8
  30.9 0.8 collective-permute-start.7
  31.6 0.5 collective-permute-start.4
  32.1 0.0 collective-permute-done.5
  32.2 0.4 collective-permute-start.3
  32.6 7.0 %all-to-all-start = ((bf16[16,48,256]{2,1,0:T(8,128)(2,1)}), bf16[16,48,256]{2,1,0:T(8,128)(2,1)S(1)}, u32[]{:S(2)}, u32[]{:S(2)}) async-start(bf16[16,48,256]{2,1,0:T(8,128)(2,1)} %bitcast.12), calls=%async_computation | async-start | bytes 786432 | tf_op jit(solution)/shard_map/all_to_all | solution.py:1112
  39.6 0.0 collective-permute-done.4
  39.6 0.0 collective-permute-done.3
  39.6 0.3 concatenate.11.own_rel
  39.9 0.0 copy-start.2
  39.9 0.1 collective-permute-start.6
  40.0 0.0 collective-permute-done.9
  40.0 0.0 collective-permute-done.8
  40.0 0.0 collective-permute-done.7
  40.0 0.1 pad_maximum_fusion.refs_0_
  40.2 0.0 copy-start.1
  40.2 2.9 %collective-permute-start.12 = (bf16[80,2432]{1,0:T(8,128)(2,1)S(1)}, bf16[80,2432]{1,0:T(8,128)(2,1)S(1)}, u32[]{:S(2)}, u32[]{:S(2)}) collective-permute-start(bf16[80,2432]{1,0:T(8,128)(2,1)S(1)} %pad_maximum_fusion.refs_0_), channel_id=1, source_target_pairs={{0,3},{1,2},{2,1},{3,0},{4,7},{5,6},{6,5},{7,4},{8,11},{9,10},{10,... | collective-permute-start | bytes 1167368 | tf_op jit(solution)/shard_map/ppermute | solution.py:944
  43.0 0.6 collective-permute-start.11
  43.6 0.1 collective-permute-start.10
  45.0 0.0 copy-done.7
  45.0 0.5 reshape.59.flags_ref
  45.6 0.0 collective-permute-done.6.other_rel
  45.6 0.7 copy-done.4
  46.3 0.0 copy-done.2
  46.3 15.5 %shard_map.341 = (f32[1,1]{1,0:T(1,128)}, f32[1,1]{1,0:T(1,128)}, f32[1,1]{1,0:T(1,128)}, f32[320,512]{1,0:T(8,128)}, bf16[768,640]{1,0:T(8,128)(2,1)}, /*index=...) custom-call(bf16[320,512]{1,0:T(8,128)(2,1)} %copy-done.2, ...), custom_call_target="tpu_custom_call" | custom-call | flops 1000000000 | bytes 20000000 | tf_op jit(solution)/shard_map/pallas_call | solution.py:963
  61.8 0.0 copy-done.1
  61.8 0.0 collective-permute-done.12.refs_3_
  61.8 1.6 %collective-permute-done.11.refs_2_ = bf16[80,2432]{1,0:T(8,128)(2,1)} collective-permute-done((bf16[80,2432]{1,0:T(8,128)(2,1)S(1)}, bf16[80,2432]{1,0:T(8,128)(2,1)}, u32[]{:S(2)}, u32[]{:S(2)}) %collective-permute-start.11) | collective-permute-done | bytes 389152 | tf_op jit(solution)/shard_map/ppermute | solution.py:944
  63.4 0.0 collective-permute-done.10.refs_1_
  63.4 0.0 all-to-all-done.refs_13_.refs_1_
  63.4 5.3 %all-to-all-start.1 = ((bf16[16,48,640]{2,1,0:T(8,128)(2,1)}), bf16[16,48,640]{2,1,0:T(8,128)(2,1)S(1)}, u32[]{:S(2)}, u32[]{:S(2)}) async-start(bf16[16,48,640]{2,1,0:T(8,128)(2,1)} %bitcast.11), calls=%async_computation.1 | async-start | bytes 1966080 | tf_op jit(solution)/shard_map/all_to_all | solution.py:1182
  68.8 23.2 %shard_map.342 = (f32[1,1080,768]{2,1,0:T(8,128)}, bf16[320,48]{1,0:T(8,128)(2,1)}, bf16[320,768]{1,0:T(8,128)(2,1)}, bf16[320,768]{1,0:T(8,128)(2,1)}, f32[1,48...) custom-call(bf16[80,2432]{1,0:T(8,128)(2,1)} %copy-done.1, ...), custom_call_target="tpu_custom_call" | custom-call | flops 3000000000 | bytes 10000000 | tf_op jit(solution)/shard_map/pallas_call | solution.py:963
  92.0 0.0 all-to-all-done.1.refs_0_
  92.0 3.7 %shard_map.343 = (f32[1,3,48,768]{3,2,1,0:T(8,128)}, f32[1,48]{1,0:T(1,128)}, f32[1,48]{1,0:T(1,128)}, f32[1,2,48]{2,1,0:T(2,128)}) custom-call(bf16[16,48,640]{2,1,0:T(8,128)(2,1)S(1)} %all-to-all-done.1.refs_0_, bf16[16,48,256]{2,1,0:T(8,128)(2,1)} %copy-done, bf16[320,48]{1,0:T(8,128)(2,1)} %get-tuple-element.114.refs_2_, ...), custom_call_target="tpu_custom_call" | custom-call | flops 1000000000 | bytes 10000000 | tf_op jit(solution)/shard_map/pallas_call | solution.py:963
  (7 shorter events, 0.0 us)
Async XLA Ops:
  14.5 10.1 %copy-start.6 = (bf16[20,512]{1,0:T(8,128)(2,1)S(1)}, bf16[20,512]{1,0:T(8,128)(2,1)}, u32[]{:S(2)}) copy-start(bf16[20,512]{1,0:T(8,128)(2,1)} %get-tuple-element.86) | copy-start | bytes 61444
  14.5 12.8 %copy-start.5 = (bf16[20,2432]{1,0:T(8,128)(2,1)S(1)}, bf16[20,2432]{1,0:T(8,128)(2,1)}, u32[]{:S(2)}) copy-start(bf16[20,2432]{1,0:T(8,128)(2,1)} %get-tuple-element.99) | copy-start | bytes 291844
  14.5 10.0 %collective-permute-start.2 = (bf16[20,512]{1,0:T(8,128)(2,1)}, bf16[20,512]{1,0:T(8,128)(2,1)S(1)}, u32[]{:S(2)}, u32[]{:S(2)}) collective-permute-start(bf16[20,512]{1,0:T(8,128)(2,1)} %get-tuple-element.86), channel_id=1, source_target_pairs={{0,12},{1,13},{2,14},{3,15},{4,8},{5,9},{6,10},{7,11},{8,4},{9,5},... | collective-permute-start | bytes 61448 | tf_op jit(solution)/shard_map/ppermute | solution.py:944
  19.6 4.9 %collective-permute-start.1 = (bf16[20,512]{1,0:T(8,128)(2,1)}, bf16[20,512]{1,0:T(8,128)(2,1)S(1)}, u32[]{:S(2)}, u32[]{:S(2)}) collective-permute-start(bf16[20,512]{1,0:T(8,128)(2,1)} %get-tuple-element.86), channel_id=1, source_target_pairs={{0,8},{1,9},{2,10},{3,11},{4,12},{5,13},{6,14},{7,15},{8,0},{9,1},... | collective-permute-start | bytes 61448 | tf_op jit(solution)/shard_map/ppermute | solution.py:944
  19.6 4.9 %collective-permute-start = (bf16[20,512]{1,0:T(8,128)(2,1)}, bf16[20,512]{1,0:T(8,128)(2,1)S(1)}, u32[]{:S(2)}, u32[]{:S(2)}) collective-permute-start(bf16[20,512]{1,0:T(8,128)(2,1)} %get-tuple-element.86), channel_id=1, source_target_pairs={{0,4},{1,5},{2,6},{3,7},{4,0},{5,1},{6,2},{7,3},{8,12},{9,13},{10,... | collective-permute-start | bytes 61448 | tf_op jit(solution)/shard_map/ppermute | solution.py:944
  20.3 24.8 %copy-start.7 = (s32[320]{0:T(512)S(1)}, s32[320]{0:T(512)}, u32[]{:S(2)}) copy-start(s32[320]{0:T(512)} %param.23) | copy-start | bytes 3844
  24.6 7.6 %collective-permute-start.5 = (bf16[80,512]{1,0:T(8,128)(2,1)S(1)}, bf16[80,512]{1,0:T(8,128)(2,1)S(1)}, u32[]{:S(2)}, u32[]{:S(2)}) collective-permute-start(bf16[80,512]{1,0:T(8,128)(2,1)S(1)} %pad_maximum_fusion.1), channel_id=1, source_target_pairs={{0,3},{1,2},{2,1},{3,0},{4,7},{5,6},{6,5},{7,4},{8,11},{9,10},{10,... | collective-permute-start | bytes 245768 | tf_op jit(solution)/shard_map/ppermute | solution.py:944
  27.3 12.8 %collective-permute-start.9 = (bf16[20,2432]{1,0:T(8,128)(2,1)S(1)}, bf16[20,2432]{1,0:T(8,128)(2,1)S(1)}, u32[]{:S(2)}, u32[]{:S(2)}) collective-permute-start(bf16[20,2432]{1,0:T(8,128)(2,1)S(1)} %copy-done.5), channel_id=1, source_target_pairs={{0,12},{1,13},{2,14},{3,15},{4,8},{5,9},{6,10},{7,11},{8,4},{9,5},... | collective-permute-start | bytes 291848 | tf_op jit(solution)/shard_map/ppermute | solution.py:944
  30.9 9.2 %collective-permute-start.8 = (bf16[20,2432]{1,0:T(8,128)(2,1)S(1)}, bf16[20,2432]{1,0:T(8,128)(2,1)S(1)}, u32[]{:S(2)}, u32[]{:S(2)}) collective-permute-start(bf16[20,2432]{1,0:T(8,128)(2,1)S(1)} %copy-done.5), channel_id=1, source_target_pairs={{0,8},{1,9},{2,10},{3,11},{4,12},{5,13},{6,14},{7,15},{8,0},{9,1},... | collective-permute-start | bytes 291848 | tf_op jit(solution)/shard_map/ppermute | solution.py:944
  30.9 9.2 %collective-permute-start.7 = (bf16[20,2432]{1,0:T(8,128)(2,1)S(1)}, bf16[20,2432]{1,0:T(8,128)(2,1)S(1)}, u32[]{:S(2)}, u32[]{:S(2)}) collective-permute-start(bf16[20,2432]{1,0:T(8,128)(2,1)S(1)} %copy-done.5), channel_id=1, source_target_pairs={{0,4},{1,5},{2,6},{3,7},{4,0},{5,1},{6,2},{7,3},{8,12},{9,13},{10,... | collective-permute-start | bytes 291848 | tf_op jit(solution)/shard_map/ppermute | solution.py:944
  31.6 7.9 %collective-permute-start.4 = (bf16[80,512]{1,0:T(8,128)(2,1)S(1)}, bf16[80,512]{1,0:T(8,128)(2,1)S(1)}, u32[]{:S(2)}, u32[]{:S(2)}) collective-permute-start(bf16[80,512]{1,0:T(8,128)(2,1)S(1)} %pad_maximum_fusion.1), channel_id=1, source_target_pairs={{0,2},{1,3},{2,0},{3,1},{4,6},{5,7},{6,4},{7,5},{8,10},{9,11},{10,... | collective-permute-start | bytes 245768 | tf_op jit(solution)/shard_map/ppermute | solution.py:944
  32.2 7.4 %collective-permute-start.3 = (bf16[80,512]{1,0:T(8,128)(2,1)S(1)}, bf16[80,512]{1,0:T(8,128)(2,1)S(1)}, u32[]{:S(2)}, u32[]{:S(2)}) collective-permute-start(bf16[80,512]{1,0:T(8,128)(2,1)S(1)} %pad_maximum_fusion.1), channel_id=1, source_target_pairs={{0,1},{1,0},{2,3},{3,2},{4,5},{5,4},{6,7},{7,6},{8,9},{9,8},{10,11... | collective-permute-start | bytes 245768 | tf_op jit(solution)/shard_map/ppermute | solution.py:944
  32.6 30.8 %all-to-all-start = ((bf16[16,48,256]{2,1,0:T(8,128)(2,1)}), bf16[16,48,256]{2,1,0:T(8,128)(2,1)S(1)}, u32[]{:S(2)}, u32[]{:S(2)}) async-start(bf16[16,48,256]{2,1,0:T(8,128)(2,1)} %bitcast.12), calls=%async_computation | async-start | bytes 786432 | tf_op jit(solution)/shard_map/all_to_all | solution.py:1112
  39.9 6.4 %copy-start.2 = (bf16[320,512]{1,0:T(8,128)(2,1)}, bf16[320,512]{1,0:T(8,128)(2,1)S(1)}, u32[]{:S(2)}) copy-start(bf16[320,512]{1,0:T(8,128)(2,1)S(1)} %concatenate.11.own_rel) | copy-start | bytes 983044
  39.9 5.6 %collective-permute-start.6 = (bf16[320,512]{1,0:T(8,128)(2,1)S(1)}, bf16[320,512]{1,0:T(8,128)(2,1)S(1)}, u32[]{:S(2)}, u32[]{:S(2)}) collective-permute-start(bf16[320,512]{1,0:T(8,128)(2,1)S(1)} %concatenate.11.own_rel), channel_id=1, source_target_pairs={{0,16},{16,0},{1,17},{17,1},{2,18},{18,2},{3,19},{19,3},{4,20},{20... | collective-permute-start | bytes 983048 | tf_op jit(solution)/shard_map/ppermute | solution.py:1113
  40.2 21.6 %copy-start.1 = (bf16[80,2432]{1,0:T(8,128)(2,1)}, bf16[80,2432]{1,0:T(8,128)(2,1)S(1)}, u32[]{:S(2)}) copy-start(bf16[80,2432]{1,0:T(8,128)(2,1)S(1)} %pad_maximum_fusion.refs_0_) | copy-start | bytes 1167364
  40.2 21.6 %collective-permute-start.12 = (bf16[80,2432]{1,0:T(8,128)(2,1)S(1)}, bf16[80,2432]{1,0:T(8,128)(2,1)S(1)}, u32[]{:S(2)}, u32[]{:S(2)}) collective-permute-start(bf16[80,2432]{1,0:T(8,128)(2,1)S(1)} %pad_maximum_fusion.refs_0_), channel_id=1, source_target_pairs={{0,3},{1,2},{2,1},{3,0},{4,7},{5,6},{6,5},{7,4},{8,11},{9,10},{10,... | collective-permute-start | bytes 1167368 | tf_op jit(solution)/shard_map/ppermute | solution.py:944
  43.0 20.3 %collective-permute-start.11 = (bf16[80,2432]{1,0:T(8,128)(2,1)S(1)}, bf16[80,2432]{1,0:T(8,128)(2,1)}, u32[]{:S(2)}, u32[]{:S(2)}) collective-permute-start(bf16[80,2432]{1,0:T(8,128)(2,1)S(1)} %pad_maximum_fusion.refs_0_), channel_id=1, source_target_pairs={{0,2},{1,3},{2,0},{3,1},{4,6},{5,7},{6,4},{7,5},{8,10},{9,11},{10,... | collective-permute-start | bytes 1167368 | tf_op jit(solution)/shard_map/ppermute | solution.py:944
  43.6 19.8 %collective-permute-start.10 = (bf16[80,2432]{1,0:T(8,128)(2,1)S(1)}, bf16[80,2432]{1,0:T(8,128)(2,1)}, u32[]{:S(2)}, u32[]{:S(2)}) collective-permute-start(bf16[80,2432]{1,0:T(8,128)(2,1)S(1)} %pad_maximum_fusion.refs_0_), channel_id=1, source_target_pairs={{0,1},{1,0},{2,3},{3,2},{4,5},{5,4},{6,7},{7,6},{8,9},{9,8},{10,11... | collective-permute-start | bytes 1167368 | tf_op jit(solution)/shard_map/ppermute | solution.py:944
  45.6 0.7 copy-start.4
  61.8 7.0 %copy-start.3 = (bf16[80,2432]{1,0:T(8,128)(2,1)}, bf16[80,2432]{1,0:T(8,128)(2,1)S(1)}, u32[]{:S(2)}) copy-start(bf16[80,2432]{1,0:T(8,128)(2,1)S(1)} %collective-permute-done.12.refs_3_) | copy-start | bytes 1167364
  63.4 5.4 %copy-start = (bf16[16,48,256]{2,1,0:T(8,128)(2,1)}, bf16[16,48,256]{2,1,0:T(8,128)(2,1)S(1)}, u32[]{:S(2)}) copy-start(bf16[16,48,256]{2,1,0:T(8,128)(2,1)S(1)} %all-to-all-done.refs_13_.refs_1_) | copy-start | bytes 1179652
  63.4 28.6 %all-to-all-start.1 = ((bf16[16,48,640]{2,1,0:T(8,128)(2,1)}), bf16[16,48,640]{2,1,0:T(8,128)(2,1)S(1)}, u32[]{:S(2)}, u32[]{:S(2)}) async-start(bf16[16,48,640]{2,1,0:T(8,128)(2,1)} %bitcast.11), calls=%async_computation.1 | async-start | bytes 1966080 | tf_op jit(solution)/shard_map/all_to_all | solution.py:1182

commit v3 on v2

--- a/solution.py
+++ b/solution.py
@@ -17,6 +17,7 @@
 VMEM_LIMIT = 62 * 1024 * 1024
 CHUNK = 1024
 NORM_ROWS = 272
+STREAM_ROWS = 544
 PROJECT_ROWS = 1088
 
 
@@ -183,7 +184,7 @@
     hat_hbm,
     inv_hbm,
     probs_hbm,
-    query_ref,
+    keys_ref,
     embedded_ref,
     pooled_ref,
     middle_ref,
@@ -305,7 +306,7 @@
     unit_ref[...] = (
         embedded * lax.rsqrt(jnp.sum(embedded * embedded, axis=-1, keepdims=True) + 1e-06)
     ).astype(BF16)
-    query_ref[...] = query
+    keys_ref[...] = mm_nt(wide, s_triple[1]).astype(BF16)
     for copy in (put_hat, put_inv, put_probs):
         copy.wait()
 
@@ -317,19 +318,13 @@
     ab,
     hat_ref,
     probs_ref,
-    query_ref,
-    triple_hbm,
     turned_ref,
     spread_ref,
-    keys_ref,
     hat_rows_ref,
-    s_weight,
     s_turn,
-    sems,
 ):
     pairs, tokens, full_width, full_hidden = dims
     is_text, width, mask = tower_sizes(full_width, full_hidden)
-    get_weight = fetch(triple_hbm.at[0, 1], s_weight, sems.at[0])
     rows = probs_ref.shape[0]
     low = probs_ref[...]
     spread = mm(low, hat_ref[...])
@@ -340,10 +335,6 @@
     turned_ref[...] = s_turn[...].T.astype(BF16)
     pick = one_hot(iota((pairs, tokens), 1).astype(F32) == pooled_spots(ends_ref, is_text, pairs, 1))
     hat_rows_ref[...] = mm(pick, hat_ref[...]).astype(BF16)
-    wide = mm(repeat_rows(rows, pairs), query_ref[...])
-    wide = jnp.where(head_mask(rows, pairs, full_width), wide, 0.0).astype(BF16)
-    get_weight.wait()
-    keys_ref[...] = mm_nt(wide, s_weight[...]).astype(BF16)
 
 
 def in_order(pieces, stages, pairs, block, at):
@@ -689,7 +680,7 @@
     def put(at, count):
         spot = pl.ds(at, count)
         return pltpu.make_async_copy(
-            s_out.at[spot, :], out_hbm.at[0, spot, :], out_sems.at[at // NORM_ROWS]
+            s_out.at[spot, :], out_hbm.at[0, spot, :], out_sems.at[at // STREAM_ROWS]
         )
 
     def norm_rows(at, count):
@@ -704,7 +695,7 @@
         ) + mm_tn(s_left[2 * rows :, spot], middle_parts)
         put(at, count).start()
 
-    over_tokens(tokens, NORM_ROWS, norm_rows)
+    over_tokens(tokens, STREAM_ROWS, norm_rows)
     for ref in (embed_ref, narrow_ref, widen_ref, mixer_ref, widen_bias_ref, s_vectors):
         ref[...] = jnp.zeros_like(ref)
     lane = iota((full_width, slice_width), 0)
@@ -793,7 +784,7 @@
         for chunk in range(full_hidden // CHUNK):
             hidden.wait(chunk)
     over_blocks(all_pairs // block, part)
-    over_tokens(tokens, NORM_ROWS, lambda at, count: put(at, count).wait())
+    over_tokens(tokens, STREAM_ROWS, lambda at, count: put(at, count).wait())
     count = means_ref.shape[0]
     if count <= 16 and slice_width % 16 == 0:
         from_heads(
@@ -1025,7 +1016,7 @@
         hat,
         invert,
         probs,
-        query,
+        keys,
         embedded,
         pooled,
         middle,
@@ -1057,7 +1048,7 @@
             ((tokens, width), BF16),
             ((tokens, 128), F32),
             ((rows, tokens), BF16),
-            ((pairs, width), BF16),
+            ((rows, width), BF16),
             ((pairs, emb), F32),
             ((pairs, width), F32),
             ((pairs, width), F32),
@@ -1082,21 +1073,17 @@
         out_hbm=(2, 3, 4),
         cost=(10**9, 20 * 10**6),
     )
-    turned, spread, keys, hat_rows = call(
+    turned, spread, hat_rows = call(
         partial(means_kernel, dims),
-        (ends, attention_gain, attention_bias, hat, probs, query, triple_weight),
+        (ends, attention_gain, attention_bias, hat, probs),
         [
             ((width, lanes), BF16),
-            ((rows, width), BF16),
             ((rows, width), BF16),
             ((pairs, width), BF16),
         ],
         [
-            pltpu.VMEM((width, width), BF16),
             pltpu.VMEM((lanes, width), F32),
-            dma((1,)),
         ],
-        in_hbm=(6,),
         cost=(10**9, 5 * 10**6),
     )
     early_rows, own_rel = early, unit
@@ -1268,7 +1255,7 @@
             pltpu.VMEM((width // HEAD * slice_width if compact else 16, all_pairs), BF16),
             dma((7 + ahead,)),
             dma((2, chunk_count)),
-            dma((-(-tokens // NORM_ROWS),)),
+            dma((-(-tokens // STREAM_ROWS),)),
         ],
         in_hbm=tuple(range(ahead)) + tuple(ahead + index for index in (1, 2, 3, 10, 13, 15, 19, 21, 24)),
         out_hbm=(0,),

time: 96.2 us -> 95.5 us (level)
  waiting for transfers between devices: 1.66 us -> 2.76 us
  transfers between devices with their start and end apart: 15 -> 15, of which waited for: 1 -> 3; matrix products, arithmetic and copies ran while one was open for 1% -> 1% of each run, Pallas kernels for 45% -> 44%
where the time goes in v3:
time: 95.5 us; the launch traced here: 95 us
  Pallas kernels  59.5 us (62%)
  starting transfers between devices  28.8 us (30%)
  waiting for transfers between devices  2.76 us (3%)
  between operations  2.16 us (2%)
  local copies, waits for them, and re-layouts  1.62 us (2%)
    pallas_call x5, Pallas kernels, call(): pl.pallas_call(kernel, out_shape=[jax.ShapeDtypeStruct(shape, kind) for s...  59.5 us
    ppermute x12, starting transfers between devices, exchange(): parts.append(lax.ppermute(block, axis, route))  17.3 us
    all_to_all x1, starting transfers between devices, body(): lax.all_to_all(turned, 'dp', 0, 0, tiled=True)  6.08 us
    all_to_all x1, starting transfers between devices, body(): late_all = lax.all_to_all(late, 'dp', 0, 0, tiled=True)  5.36 us
    ppermute x12, waiting for transfers between devices, exchange(): parts.append(lax.ppermute(block, axis, route))  2.56 us
  transfers between devices with their start and end apart: 15, of which 3 were waited for; matrix products, arithmetic and copies ran while one was open for 1% of the time, Pallas kernels for 44%

profile of v3, /device:TPU:0, one launch (start us, length us, event | category | flops | bytes accessed | tf_op | source)
XLA Modules:
  0.0 95.0 jit_solution(15731674912079603753)
XLA Ops:
  0.7 14.2 %shard_map.339 = (bf16[20,512]{1,0:T(8,128)(2,1)}, bf16[20,2432]{1,0:T(8,128)(2,1)}, bf16[1080,768]{1,0:T(8,128)(2,1)}, f32[1080,128]{1,0:T(8,128)}, bf16[240,10...) custom-call(s32[1,20]{1,0:T(1,128)} %bitcast.13, ...), custom_call_target="tpu_custom_call" | custom-call | flops 1000000000 | bytes 20000000 | tf_op jit(solution)/shard_map/pallas_call | solution.py:954
  14.8 0.0 copy-start.6
  14.8 0.0 copy-start.5
  14.8 0.0 copy-start.7
  14.9 5.1 %collective-permute-start.2 = (bf16[20,512]{1,0:T(8,128)(2,1)}, bf16[20,512]{1,0:T(8,128)(2,1)S(1)}, u32[]{:S(2)}, u32[]{:S(2)}) collective-permute-start(bf16[20,512]{1,0:T(8,128)(2,1)} %get-tuple-element.84), channel_id=1, source_target_pairs={{0,12},{1,13},{2,14},{3,15},{4,8},{5,9},{6,10},{7,11},{8,4},{9,5},... | collective-permute-start | bytes 61448 | tf_op jit(solution)/shard_map/ppermute | solution.py:935
  20.0 0.0 collective-permute-start.1
  20.0 0.6 collective-permute-start
  20.6 3.3 %shard_map.340 = (bf16[768,256]{1,0:T(8,128)(2,1)}, bf16[240,768]{1,0:T(8,128)(2,1)}, bf16[20,768]{1,0:T(8,128)(2,1)}) custom-call(s32[1,20]{1,0:T(1,128)} %bitcast.14, f32[1,768]{1,0:T(1,128)} %refs_15_.1, f32[1,768]{1,0:T(1,128)} %refs_16_.1, bf16[1080,768]{1,0:T(8,128)(2,1)} %get-tuple-element.78.hat_ref.hat_hbm.refs_5_, ...), custom_call_target="tpu_custom_call" | custom-call | flops 1000000000 | bytes 5000000 | tf_op jit(solution)/shard_map/pallas_call | solution.py:954
  24.0 0.0 collective-permute-done.2
  24.0 0.9 collective-permute-done.1
  24.9 0.0 collective-permute-done
  24.9 0.0 copy-done.6
  25.0 2.5 %collective-permute-start.5 = (bf16[80,512]{1,0:T(8,128)(2,1)S(1)}, bf16[80,512]{1,0:T(8,128)(2,1)S(1)}, u32[]{:S(2)}, u32[]{:S(2)}) collective-permute-start(bf16[80,512]{1,0:T(8,128)(2,1)S(1)} %pad_maximum_fusion.1), channel_id=1, source_target_pairs={{0,3},{1,2},{2,1},{3,0},{4,7},{5,6},{6,5},{7,4},{8,11},{9,10},{10,... | collective-permute-start | bytes 245768 | tf_op jit(solution)/shard_map/ppermute | solution.py:935
  27.5 0.0 copy-done.5
  27.5 2.8 %collective-permute-start.9 = (bf16[20,2432]{1,0:T(8,128)(2,1)S(1)}, bf16[20,2432]{1,0:T(8,128)(2,1)S(1)}, u32[]{:S(2)}, u32[]{:S(2)}) collective-permute-start(bf16[20,2432]{1,0:T(8,128)(2,1)S(1)} %copy-done.5), channel_id=1, source_target_pairs={{0,12},{1,13},{2,14},{3,15},{4,8},{5,9},{6,10},{7,11},{8,4},{9,5},... | collective-permute-start | bytes 291848 | tf_op jit(solution)/shard_map/ppermute | solution.py:935
  30.3 0.0 collective-permute-start.8
  30.3 1.6 %collective-permute-start.7 = (bf16[20,2432]{1,0:T(8,128)(2,1)S(1)}, bf16[20,2432]{1,0:T(8,128)(2,1)S(1)}, u32[]{:S(2)}, u32[]{:S(2)}) collective-permute-start(bf16[20,2432]{1,0:T(8,128)(2,1)S(1)} %copy-done.5), channel_id=1, source_target_pairs={{0,4},{1,5},{2,6},{3,7},{4,0},{5,1},{6,2},{7,3},{8,12},{9,13},{10,... | collective-permute-start | bytes 291848 | tf_op jit(solution)/shard_map/ppermute | solution.py:935
  31.9 0.5 collective-permute-start.4
  32.4 0.0 collective-permute-done.5
  32.4 0.5 collective-permute-start.3
  32.9 6.1 %all-to-all-start = ((bf16[16,48,256]{2,1,0:T(8,128)(2,1)}), bf16[16,48,256]{2,1,0:T(8,128)(2,1)S(1)}, u32[]{:S(2)}, u32[]{:S(2)}) async-start(bf16[16,48,256]{2,1,0:T(8,128)(2,1)} %bitcast.12), calls=%async_computation | async-start | bytes 786432 | tf_op jit(solution)/shard_map/all_to_all | solution.py:1099
  39.0 0.0 collective-permute-done.4
  39.0 0.0 collective-permute-done.3
  39.0 0.3 concatenate.11.own_rel
  39.3 0.0 copy-start.2
  39.4 0.1 collective-permute-start.6
  39.4 0.0 collective-permute-done.9
  39.4 0.0 collective-permute-done.8
  39.5 0.0 collective-permute-done.7
  39.5 0.1 pad_maximum_fusion.refs_0_
  39.6 2.9 %collective-permute-start.12 = (bf16[80,2432]{1,0:T(8,128)(2,1)S(1)}, bf16[80,2432]{1,0:T(8,128)(2,1)S(1)}, u32[]{:S(2)}, u32[]{:S(2)}) collective-permute-start(bf16[80,2432]{1,0:T(8,128)(2,1)S(1)} %pad_maximum_fusion.refs_0_), channel_id=1, source_target_pairs={{0,3},{1,2},{2,1},{3,0},{4,7},{5,6},{6,5},{7,4},{8,11},{9,10},{10,... | collective-permute-start | bytes 1167368 | tf_op jit(solution)/shard_map/ppermute | solution.py:935
  42.5 0.6 collective-permute-start.11
  43.0 0.1 collective-permute-start.10
  44.4 0.0 copy-done.7
  44.4 0.5 reshape.59.flags_ref
  45.0 0.0 collective-permute-done.6.other_rel
  45.0 0.7 copy-done.4
  45.7 15.5 %shard_map.341 = (f32[1,1]{1,0:T(1,128)}, f32[1,1]{1,0:T(1,128)}, f32[1,1]{1,0:T(1,128)}, f32[320,512]{1,0:T(8,128)}, bf16[768,640]{1,0:T(8,128)(2,1)}, /*index=...) custom-call(bf16[320,512]{1,0:T(8,128)(2,1)} %copy-done.2, ...), custom_call_target="tpu_custom_call" | custom-call | flops 1000000000 | bytes 20000000 | tf_op jit(solution)/shard_map/pallas_call | solution.py:954
  61.2 0.0 collective-permute-done.12.refs_3_
  61.2 1.6 %collective-permute-done.11.refs_2_ = bf16[80,2432]{1,0:T(8,128)(2,1)} collective-permute-done((bf16[80,2432]{1,0:T(8,128)(2,1)S(1)}, bf16[80,2432]{1,0:T(8,128)(2,1)}, u32[]{:S(2)}, u32[]{:S(2)}) %collective-permute-start.11) | collective-permute-done | bytes 389152 | tf_op jit(solution)/shard_map/ppermute | solution.py:935
  62.8 0.0 collective-permute-done.10.refs_1_
  62.8 0.0 all-to-all-done.refs_13_.refs_1_
  62.8 5.4 %all-to-all-start.1 = ((bf16[16,48,640]{2,1,0:T(8,128)(2,1)}), bf16[16,48,640]{2,1,0:T(8,128)(2,1)S(1)}, u32[]{:S(2)}, u32[]{:S(2)}) async-start(bf16[16,48,640]{2,1,0:T(8,128)(2,1)} %bitcast.11), calls=%async_computation.1 | async-start | bytes 1966080 | tf_op jit(solution)/shard_map/all_to_all | solution.py:1169
  68.2 0.0 copy-done.3
  68.2 0.0 copy-done
  68.2 22.9 %shard_map.342 = (f32[1,1080,768]{2,1,0:T(8,128)}, bf16[320,48]{1,0:T(8,128)(2,1)}, bf16[320,768]{1,0:T(8,128)(2,1)}, bf16[320,768]{1,0:T(8,128)(2,1)}, f32[1,48...) custom-call(bf16[80,2432]{1,0:T(8,128)(2,1)} %copy-done.1, ...), custom_call_target="tpu_custom_call" | custom-call | flops 3000000000 | bytes 10000000 | tf_op jit(solution)/shard_map/pallas_call | solution.py:954
  91.1 0.2 all-to-all-done.1.refs_0_
  91.3 3.7 %shard_map.343 = (f32[1,3,48,768]{3,2,1,0:T(8,128)}, f32[1,48]{1,0:T(1,128)}, f32[1,48]{1,0:T(1,128)}, f32[1,2,48]{2,1,0:T(2,128)}) custom-call(bf16[16,48,640]{2,1,0:T(8,128)(2,1)S(1)} %all-to-all-done.1.refs_0_, bf16[16,48,256]{2,1,0:T(8,128)(2,1)} %copy-done, bf16[320,48]{1,0:T(8,128)(2,1)} %get-tuple-element.112.refs_2_, ...), custom_call_target="tpu_custom_call" | custom-call | flops 1000000000 | bytes 10000000 | tf_op jit(solution)/shard_map/pallas_call | solution.py:954
  (7 shorter events, 0.0 us)
Async XLA Ops:
  14.8 10.1 %copy-start.6 = (bf16[20,512]{1,0:T(8,128)(2,1)S(1)}, bf16[20,512]{1,0:T(8,128)(2,1)}, u32[]{:S(2)}) copy-start(bf16[20,512]{1,0:T(8,128)(2,1)} %get-tuple-element.84) | copy-start | bytes 61444
  14.8 12.6 %copy-start.5 = (bf16[20,2432]{1,0:T(8,128)(2,1)S(1)}, bf16[20,2432]{1,0:T(8,128)(2,1)}, u32[]{:S(2)}) copy-start(bf16[20,2432]{1,0:T(8,128)(2,1)} %get-tuple-element.97) | copy-start | bytes 291844
  14.8 29.6 %copy-start.7 = (s32[320]{0:T(512)S(1)}, s32[320]{0:T(512)}, u32[]{:S(2)}) copy-start(s32[320]{0:T(512)} %param.23) | copy-start | bytes 3844
  14.9 9.1 %collective-permute-start.2 = (bf16[20,512]{1,0:T(8,128)(2,1)}, bf16[20,512]{1,0:T(8,128)(2,1)S(1)}, u32[]{:S(2)}, u32[]{:S(2)}) collective-permute-start(bf16[20,512]{1,0:T(8,128)(2,1)} %get-tuple-element.84), channel_id=1, source_target_pairs={{0,12},{1,13},{2,14},{3,15},{4,8},{5,9},{6,10},{7,11},{8,4},{9,5},... | collective-permute-start | bytes 61448 | tf_op jit(solution)/shard_map/ppermute | solution.py:935
  20.0 4.9 %collective-permute-start.1 = (bf16[20,512]{1,0:T(8,128)(2,1)}, bf16[20,512]{1,0:T(8,128)(2,1)S(1)}, u32[]{:S(2)}, u32[]{:S(2)}) collective-permute-start(bf16[20,512]{1,0:T(8,128)(2,1)} %get-tuple-element.84), channel_id=1, source_target_pairs={{0,8},{1,9},{2,10},{3,11},{4,12},{5,13},{6,14},{7,15},{8,0},{9,1},... | collective-permute-start | bytes 61448 | tf_op jit(solution)/shard_map/ppermute | solution.py:935
  20.0 4.9 %collective-permute-start = (bf16[20,512]{1,0:T(8,128)(2,1)}, bf16[20,512]{1,0:T(8,128)(2,1)S(1)}, u32[]{:S(2)}, u32[]{:S(2)}) collective-permute-start(bf16[20,512]{1,0:T(8,128)(2,1)} %get-tuple-element.84), channel_id=1, source_target_pairs={{0,4},{1,5},{2,6},{3,7},{4,0},{5,1},{6,2},{7,3},{8,12},{9,13},{10,... | collective-permute-start | bytes 61448 | tf_op jit(solution)/shard_map/ppermute | solution.py:935
  25.0 7.4 %collective-permute-start.5 = (bf16[80,512]{1,0:T(8,128)(2,1)S(1)}, bf16[80,512]{1,0:T(8,128)(2,1)S(1)}, u32[]{:S(2)}, u32[]{:S(2)}) collective-permute-start(bf16[80,512]{1,0:T(8,128)(2,1)S(1)} %pad_maximum_fusion.1), channel_id=1, source_target_pairs={{0,3},{1,2},{2,1},{3,0},{4,7},{5,6},{6,5},{7,4},{8,11},{9,10},{10,... | collective-permute-start | bytes 245768 | tf_op jit(solution)/shard_map/ppermute | solution.py:935
  27.5 12.0 %collective-permute-start.9 = (bf16[20,2432]{1,0:T(8,128)(2,1)S(1)}, bf16[20,2432]{1,0:T(8,128)(2,1)S(1)}, u32[]{:S(2)}, u32[]{:S(2)}) collective-permute-start(bf16[20,2432]{1,0:T(8,128)(2,1)S(1)} %copy-done.5), channel_id=1, source_target_pairs={{0,12},{1,13},{2,14},{3,15},{4,8},{5,9},{6,10},{7,11},{8,4},{9,5},... | collective-permute-start | bytes 291848 | tf_op jit(solution)/shard_map/ppermute | solution.py:935
  30.3 9.2 %collective-permute-start.8 = (bf16[20,2432]{1,0:T(8,128)(2,1)S(1)}, bf16[20,2432]{1,0:T(8,128)(2,1)S(1)}, u32[]{:S(2)}, u32[]{:S(2)}) collective-permute-start(bf16[20,2432]{1,0:T(8,128)(2,1)S(1)} %copy-done.5), channel_id=1, source_target_pairs={{0,8},{1,9},{2,10},{3,11},{4,12},{5,13},{6,14},{7,15},{8,0},{9,1},... | collective-permute-start | bytes 291848 | tf_op jit(solution)/shard_map/ppermute | solution.py:935
  30.3 9.2 %collective-permute-start.7 = (bf16[20,2432]{1,0:T(8,128)(2,1)S(1)}, bf16[20,2432]{1,0:T(8,128)(2,1)S(1)}, u32[]{:S(2)}, u32[]{:S(2)}) collective-permute-start(bf16[20,2432]{1,0:T(8,128)(2,1)S(1)} %copy-done.5), channel_id=1, source_target_pairs={{0,4},{1,5},{2,6},{3,7},{4,0},{5,1},{6,2},{7,3},{8,12},{9,13},{10,... | collective-permute-start | bytes 291848 | tf_op jit(solution)/shard_map/ppermute | solution.py:935
  31.9 7.1 %collective-permute-start.4 = (bf16[80,512]{1,0:T(8,128)(2,1)S(1)}, bf16[80,512]{1,0:T(8,128)(2,1)S(1)}, u32[]{:S(2)}, u32[]{:S(2)}) collective-permute-start(bf16[80,512]{1,0:T(8,128)(2,1)S(1)} %pad_maximum_fusion.1), channel_id=1, source_target_pairs={{0,2},{1,3},{2,0},{3,1},{4,6},{5,7},{6,4},{7,5},{8,10},{9,11},{10,... | collective-permute-start | bytes 245768 | tf_op jit(solution)/shard_map/ppermute | solution.py:935
  32.4 6.6 %collective-permute-start.3 = (bf16[80,512]{1,0:T(8,128)(2,1)S(1)}, bf16[80,512]{1,0:T(8,128)(2,1)S(1)}, u32[]{:S(2)}, u32[]{:S(2)}) collective-permute-start(bf16[80,512]{1,0:T(8,128)(2,1)S(1)} %pad_maximum_fusion.1), channel_id=1, source_target_pairs={{0,1},{1,0},{2,3},{3,2},{4,5},{5,4},{6,7},{7,6},{8,9},{9,8},{10,11... | collective-permute-start | bytes 245768 | tf_op jit(solution)/shard_map/ppermute | solution.py:935
  32.9 29.9 %all-to-all-start = ((bf16[16,48,256]{2,1,0:T(8,128)(2,1)}), bf16[16,48,256]{2,1,0:T(8,128)(2,1)S(1)}, u32[]{:S(2)}, u32[]{:S(2)}) async-start(bf16[16,48,256]{2,1,0:T(8,128)(2,1)} %bitcast.12), calls=%async_computation | async-start | bytes 786432 | tf_op jit(solution)/shard_map/all_to_all | solution.py:1099
  39.3 6.4 %copy-start.2 = (bf16[320,512]{1,0:T(8,128)(2,1)}, bf16[320,512]{1,0:T(8,128)(2,1)S(1)}, u32[]{:S(2)}) copy-start(bf16[320,512]{1,0:T(8,128)(2,1)S(1)} %concatenate.11.own_rel) | copy-start | bytes 983044
  39.4 5.6 %collective-permute-start.6 = (bf16[320,512]{1,0:T(8,128)(2,1)S(1)}, bf16[320,512]{1,0:T(8,128)(2,1)S(1)}, u32[]{:S(2)}, u32[]{:S(2)}) collective-permute-start(bf16[320,512]{1,0:T(8,128)(2,1)S(1)} %concatenate.11.own_rel), channel_id=1, source_target_pairs={{0,16},{16,0},{1,17},{17,1},{2,18},{18,2},{3,19},{19,3},{4,20},{20... | collective-permute-start | bytes 983048 | tf_op jit(solution)/shard_map/ppermute | solution.py:1100
  39.6 21.6 %copy-start.1 = (bf16[80,2432]{1,0:T(8,128)(2,1)}, bf16[80,2432]{1,0:T(8,128)(2,1)S(1)}, u32[]{:S(2)}) copy-start(bf16[80,2432]{1,0:T(8,128)(2,1)S(1)} %pad_maximum_fusion.refs_0_) | copy-start | bytes 1167364
  39.6 21.6 %collective-permute-start.12 = (bf16[80,2432]{1,0:T(8,128)(2,1)S(1)}, bf16[80,2432]{1,0:T(8,128)(2,1)S(1)}, u32[]{:S(2)}, u32[]{:S(2)}) collective-permute-start(bf16[80,2432]{1,0:T(8,128)(2,1)S(1)} %pad_maximum_fusion.refs_0_), channel_id=1, source_target_pairs={{0,3},{1,2},{2,1},{3,0},{4,7},{5,6},{6,5},{7,4},{8,11},{9,10},{10,... | collective-permute-start | bytes 1167368 | tf_op jit(solution)/shard_map/ppermute | solution.py:935
  42.5 20.3 %collective-permute-start.11 = (bf16[80,2432]{1,0:T(8,128)(2,1)S(1)}, bf16[80,2432]{1,0:T(8,128)(2,1)}, u32[]{:S(2)}, u32[]{:S(2)}) collective-permute-start(bf16[80,2432]{1,0:T(8,128)(2,1)S(1)} %pad_maximum_fusion.refs_0_), channel_id=1, source_target_pairs={{0,2},{1,3},{2,0},{3,1},{4,6},{5,7},{6,4},{7,5},{8,10},{9,11},{10,... | collective-permute-start | bytes 1167368 | tf_op jit(solution)/shard_map/ppermute | solution.py:935
  43.0 19.8 %collective-permute-start.10 = (bf16[80,2432]{1,0:T(8,128)(2,1)S(1)}, bf16[80,2432]{1,0:T(8,128)(2,1)}, u32[]{:S(2)}, u32[]{:S(2)}) collective-permute-start(bf16[80,2432]{1,0:T(8,128)(2,1)S(1)} %pad_maximum_fusion.refs_0_), channel_id=1, source_target_pairs={{0,1},{1,0},{2,3},{3,2},{4,5},{5,4},{6,7},{7,6},{8,9},{9,8},{10,11... | collective-permute-start | bytes 1167368 | tf_op jit(solution)/shard_map/ppermute | solution.py:935
  45.0 0.7 copy-start.4
  61.2 7.0 %copy-start.3 = (bf16[80,2432]{1,0:T(8,128)(2,1)}, bf16[80,2432]{1,0:T(8,128)(2,1)S(1)}, u32[]{:S(2)}) copy-start(bf16[80,2432]{1,0:T(8,128)(2,1)S(1)} %collective-permute-done.12.refs_3_) | copy-start | bytes 1167364
  62.8 5.4 %copy-start = (bf16[16,48,256]{2,1,0:T(8,128)(2,1)}, bf16[16,48,256]{2,1,0:T(8,128)(2,1)S(1)}, u32[]{:S(2)}) copy-start(bf16[16,48,256]{2,1,0:T(8,128)(2,1)S(1)} %all-to-all-done.refs_13_.refs_1_) | copy-start | bytes 1179652
  62.8 28.5 %all-to-all-start.1 = ((bf16[16,48,640]{2,1,0:T(8,128)(2,1)}), bf16[16,48,640]{2,1,0:T(8,128)(2,1)S(1)}, u32[]{:S(2)}, u32[]{:S(2)}) async-start(bf16[16,48,640]{2,1,0:T(8,128)(2,1)} %bitcast.11), calls=%async_computation.1 | async-start | bytes 1966080 | tf_op jit(solution)/shard_map/all_to_all | solution.py:1169
